TPU v7x, 32 devices: a whole 2x2x4 slice. The times are simulated.
32 devices in a mesh: col: 8 (over z, y), row: 4 (over x, core).
Axes of the slice: x: 2, y: 2, z: 4, core: 2. Of those that a mesh axis runs over, the one named last changes fastest.
Arguments:
- tile_left: bfloat16 [8, 8, 1024, 64], P('col', 'row'), may hold values from -0.41992188 to 0.41992188
- tile_right: bfloat16 [8, 8, 1024, 64], P('col', 'row'), may hold values from -0.1875 to 0.1875
- row_left: bfloat16 [8, 1024, 64], P('col'), may hold values from -0.41992188 to 0.41992188
- row_right: bfloat16 [8, 1024, 64], P('col'), may hold values from -0.1875 to 0.1875
- sketch: bfloat16 [1024, 64], replicated, may hold values from -6 to 6
- panel_left: bfloat16 [8, 1024, 64], P('row'), may hold values from -0.375 to 0.375
- panel_right: bfloat16 [8, 1024, 64], P('row'), may hold values from -0.1875 to 0.1875
- pivot_inverse: bfloat16 [1024, 1024], replicated, as said below
- band_inverse: bfloat16 [8, 1024, 1024], P('row'), as said below
- link_left: bfloat16 [8, 1024, 64], P('row'), may hold values from -0.75 to 0.75
- link_right: bfloat16 [8, 1024, 64], P('row'), may hold values from -0.0625 to 0.0625
- pivot_rhs: bfloat16 [1024, 4096], P(None, 'col'), may hold values from -6 to 6
- band_rhs: bfloat16 [8, 1024, 4096], P('row', None, 'col'), may hold values from -6 to 6
- carry_in: float32 [64, 4096], P(None, 'col'), may hold values from -3 to 3
Outputs:
- pivot_solution: bfloat16 [1024, 4096], P(None, 'col')
- schur_right: float32 [8, 1024, 64], P('row', 'col')
- band_solution: bfloat16 [8, 1024, 4096], P('row', None, 'col')
- link_states: float32 [8, 64, 4096], P('row', None, 'col')
Inputs may be any that keep to these rules, and one draw needn't show every extreme that they name: `pivot_inverse`: each tile is lower triangular with a positive diagonal, the inverse of a Cholesky factor of a diagonal covariance tile. `band_inverse`: each tile is lower triangular with a positive diagonal, the inverse of a Cholesky factor of a diagonal covariance tile.
All inputs are finite; a program needn't handle non-finite values.
Results may differ from a plain program's by a relative error of at most 0.0056.
Values sent between devices are 32-bit elements; how exact they have to be, the bound alone decides.
No kernel may reach another device: no remote copies, remote signals or barrier semaphores. Data moves between devices by JAX's collectives and lax.ppermute only.
A program may use at most 128 MiB of HBM per device.

v0:
```python
import jax
import jax.numpy as jnp
from jax import lax
from jax.sharding import PartitionSpec as P

HIGHEST_PRECISION = lax.Precision.HIGHEST


def prefix(part, axis, combine, identity):
    place = lax.axis_index(axis)
    gathered = jax.tree.map(lambda a: lax.all_gather(a, axis), part)
    state = jax.tree.map(lambda a, e: jnp.zeros_like(a) + jnp.asarray(e, a.dtype), part, identity)

    def one(lap, state):
        return combine(
            state, jax.tree.map(lambda a: lax.dynamic_index_in_dim(a, lap, 0, False), gathered)
        )

    return lax.fori_loop(0, place, one, state)


def widened(array):
    return array.astype(jnp.float32)


def lower_inverse(gram_matrix):
    gram_lower = jnp.linalg.cholesky(gram_matrix)
    identity_matrix = jnp.broadcast_to(
        jnp.eye(gram_matrix.shape[-1], dtype=jnp.float32), gram_matrix.shape
    )
    return lax.linalg.triangular_solve(gram_lower, identity_matrix, left_side=True, lower=True)


def shards(
    tile_left,
    tile_right,
    row_left,
    row_right,
    sketch,
    panel_left,
    panel_right,
    pivot_inverse,
    band_inverse,
    link_left,
    link_right,
    pivot_rhs,
    band_rhs,
    carry_in,
):
    pivot_solution = jnp.dot(pivot_inverse, pivot_rhs, preferred_element_type=jnp.float32).astype(
        jnp.bfloat16
    )
    pulled = jnp.einsum(
        "nm,nc->mc", pivot_inverse, pivot_solution, preferred_element_type=jnp.float32
    )
    coupling = jnp.einsum(
        "jbnr,jns->jbrs", tile_right, row_right, preferred_element_type=jnp.float32
    )
    probe_core = jnp.einsum("jnr,ns->jrs", row_left, sketch, preferred_element_type=jnp.float32)
    sketch_core = jnp.einsum("jbrs,jst->jbrt", coupling, probe_core, precision=HIGHEST_PRECISION)
    left_wide = widened(tile_left)
    sketch_terms = jnp.einsum("jbnr,jbrt->bnt", left_wide, sketch_core, precision=HIGHEST_PRECISION)
    sketched = lax.psum(sketch_terms, "col")
    gram_matrix = jnp.einsum("bnr,bns->brs", sketched, sketched, precision=HIGHEST_PRECISION)
    inverse_low = lower_inverse(gram_matrix)
    panel_basis = jnp.einsum("bnr,bsr->bns", sketched, inverse_low, precision=HIGHEST_PRECISION)
    projected = jnp.einsum("jbnr,bns->jbrs", left_wide, panel_basis, precision=HIGHEST_PRECISION)
    middle = jnp.einsum("jbrs,jbrt->jbst", coupling, projected, precision=HIGHEST_PRECISION)
    schur_terms = jnp.einsum(
        "jns,jbst->bnt", widened(row_left), middle, precision=HIGHEST_PRECISION
    )
    schur_full = lax.psum(schur_terms, "col")
    slab_rows = schur_full.shape[1] // lax.axis_size("col")
    schur_right = lax.dynamic_slice_in_dim(
        schur_full, lax.axis_index("col") * slab_rows, slab_rows, 1
    )
    panel_coeffs = jnp.einsum(
        "bnr,nc->brc", widened(panel_right), pulled, precision=HIGHEST_PRECISION
    )
    schur_coeffs = jnp.einsum("bnr,nc->brc", schur_full, pulled, precision=HIGHEST_PRECISION)
    panel_term = jnp.einsum(
        "bnr,brc->bnc", widened(panel_left), panel_coeffs, precision=HIGHEST_PRECISION
    ) - jnp.einsum("bnr,brc->bnc", panel_basis, schur_coeffs, precision=HIGHEST_PRECISION)
    reduced = (band_rhs.astype(jnp.float32) - panel_term).astype(jnp.bfloat16)
    local_part = jnp.einsum(
        "bnm,bmc->bnc", band_inverse, reduced, preferred_element_type=jnp.float32
    )
    feed_columns = jnp.einsum(
        "bnm,bmr->bnr", band_inverse, link_left, preferred_element_type=jnp.float32
    )
    right_wide = widened(link_right)
    band_count = band_rhs.shape[0]
    rank_count = carry_in.shape[0]
    state_gain = jnp.einsum("bnr,bns->brs", right_wide, feed_columns, precision=HIGHEST_PRECISION)
    state_offset = jnp.einsum("bnr,bnc->brc", right_wide, local_part, precision=HIGHEST_PRECISION)
    map_matrix = jnp.eye(rank_count, dtype=jnp.float32)
    map_offset = jnp.zeros(carry_in.shape, jnp.float32)
    for position in range(band_count):
        map_matrix = -jnp.dot(state_gain[position], map_matrix, precision=HIGHEST_PRECISION)
        map_offset = state_offset[position] - jnp.dot(
            state_gain[position], map_offset, precision=HIGHEST_PRECISION
        )

    def compose(earlier, later):
        return (
            jnp.dot(later[0], earlier[0], precision=HIGHEST_PRECISION),
            later[1] + jnp.dot(later[0], earlier[1], precision=HIGHEST_PRECISION),
        )

    identity_pair = (jnp.eye(rank_count, dtype=jnp.float32), jnp.zeros(carry_in.shape, jnp.float32))
    prefix_matrix, prefix_offset = prefix((map_matrix, map_offset), "row", compose, identity_pair)
    incoming = prefix_offset + jnp.dot(prefix_matrix, carry_in, precision=HIGHEST_PRECISION)
    solved_rows = []
    state_rows = []
    prior_state = incoming
    for position in range(band_count):
        solved = local_part[position] - jnp.dot(
            feed_columns[position], prior_state, precision=HIGHEST_PRECISION
        )
        prior_state = jnp.einsum(
            "nr,nc->rc", right_wide[position], solved, precision=HIGHEST_PRECISION
        )
        solved_rows.append(solved.astype(jnp.bfloat16))
        state_rows.append(prior_state)
    return (pivot_solution, schur_right, jnp.stack(solved_rows), jnp.stack(state_rows))


def solution(mesh):
    return jax.shard_map(
        shards,
        mesh=mesh,
        in_specs=(
            P("col", "row", None, None),
            P("col", "row", None, None),
            P("col", None, None),
            P("col", None, None),
            P(),
            P("row", None, None),
            P("row", None, None),
            P(),
            P("row", None, None),
            P("row", None, None),
            P("row", None, None),
            P(None, "col"),
            P("row", None, "col"),
            P(None, "col"),
        ),
        out_specs=(
            P(None, "col"),
            P("row", "col", None),
            P("row", None, "col"),
            P("row", None, "col"),
        ),
        check_vma=False,
    )
```

profile of v0, /device:TPU:3, one launch (start us, length us, event | category | flops | bytes accessed | tf_op | source)
XLA Modules:
  0.0 244.0 jit_solution(11472437861844407317)
XLA Ops:
  10.1 2.1 convolution_bitcast_fusion.1
  12.2 2.5 %convolution_convert_fusion = bf16[1024,512]{1,0:T(8,128)(2,1)S(1)} fusion(bf16[1024,1024]{1,0:T(8,128)(2,1)S(1)} %copy-done, bf16[1024,512]{1,0:T(8,128)(2,1)} %param.27), kind=kOutput, calls=%fused_computation.20 | convolution fusion | flops 1074266112 | bytes 4194304 | tf_op jit(solution)/shard_map/dot_general | solution.py:50
  17.4 2.0 fusion.13
  20.8 63.2 %all-reduce.3.cloned.1.call-done = f32[2,1024,64]{1,2,0:T(8,128)} async-done(((f32[2,1024,64]{1,2,0:T(8,128)}), f32[2,1024,64]{1,2,0:T(8,128)}) %all-reduce.3.cloned.1.call-update) | async-done | bytes 524304 | tf_op jit(solution)/shard_map/psum | solution.py:63
  84.0 1.8 fusion.36
  86.0 11.7 %custom-call.7 = f32[2,64,64]{2,1,0:T(8,128)S(1)} custom-call(f32[2,64,64]{2,1,0:T(8,128)S(1)} %fusion.30), custom_call_target="Cholesky" | custom-call | tf_op jit(solution)/shard_map/jit(cholesky)/cholesky | solution.py:27
  97.9 9.8 %custom-call.8 = f32[2,1,64,64]{2,3,1,0:T(8,128)S(1)} custom-call(f32[2,1,64,64]{3,2,1,0:T(8,128)S(1)} %select_bitcast_fusion), custom_call_target="InvertDiagBlocksLowerTriangular" | custom-call | tf_op jit(solution)/shard_map/triangular_solve | solution.py:31
  108.1 1.6 fusion.37
  111.2 2.1 convolution_bitcast_fusion
  113.7 1.9 copy.28
  116.1 8.4 %all-gather = f32[256,64]{1,0:T(8,128)} all-gather(f32[64,64]{1,0:T(8,128)S(1)} %convolution_negate_fusion), channel_id=2, replica_groups=mesh['col'=8,'row'=4] {'row'}, dimensions={0}, use_global_device_ids=true | all-gather | bytes 81920 | tf_op jit(solution)/shard_map/all_gather | solution.py:11
  124.5 60.7 %all-reduce.5.cloned.1.call-done = f32[2,1024,64]{1,2,0:T(8,128)} async-done(((f32[2,1024,64]{1,2,0:T(8,128)}), f32[2,1024,64]{1,2,0:T(8,128)}) %all-reduce.5.cloned.1.call-update) | async-done | bytes 524304 | tf_op jit(solution)/shard_map/psum | solution.py:72
  185.2 4.0 %fusion.11 = f32[2,64,512]{2,1,0:T(8,128)S(1)} fusion(f32[2,1024,64]{1,2,0:T(8,128)} %all-reduce.5.cloned.1.call-done, f32[512,1024]{1,0:T(8,128)} %copy-done.1), kind=kOutput, calls=%fused_computation.16 | convolution fusion | flops 805306368 | bytes 2883584 | tf_op jit(solution)/shard_map/bnr,nc->brc/dot_general | solution.py:80
  189.2 3.5 %fusion.40 = f32[2,1024,512]{2,1,0:T(8,128)S(1)} fusion(f32[2,1024,64]{1,2,0:T(8,128)S(1)} %fusion.37, f32[2,64,512]{2,1,0:T(8,128)S(1)} %fusion.11), kind=kOutput, calls=%fused_computation.74 | convolution fusion | flops 805306368 | bytes 4980736 | tf_op jit(solution)/shard_map/bnr,brc->bnc/dot_general | solution.py:83
  192.8 2.3 fusion.8
  195.1 2.9 %fusion.41 = f32[2,512,1024]{2,1,0:T(8,128)S(1)} fusion(bf16[2,1024,512]{2,1,0:T(8,128)(2,1)S(1)} %fusion.8, bf16[2,1024,1024]{2,1,0:T(8,128)(2,1)S(1)} %copy-done.5), kind=kOutput, calls=%fused_computation.75 | convolution fusion | flops 2147483648 | bytes 10485760 | tf_op jit(solution)/shard_map/bnm,bmc->bnc/dot_general | solution.py:85
  198.0 2.5 %convolution_bitcast_fusion.2 = f32[2,64,512]{2,1,0:T(8,128)S(1)} fusion(f32[2,512,1024]{2,1,0:T(8,128)S(1)} %fusion.41, bf16[2,1024,64]{1,2,0:T(8,128)(2,1)S(1)} %copy-done.6), kind=kOutput, calls=%fused_computation.23 | convolution fusion | flops 805306368 | bytes 4718592 | tf_op jit(solution)/shard_map/bnr,bnc->brc/dot_general | solution.py:95
  201.1 8.8 %all-gather.1 = f32[256,512]{1,0:T(8,128)S(1)} all-gather(f32[64,512]{1,0:T(8,128)S(1)} %convolution_subtract_fusion), channel_id=3, replica_groups=mesh['col'=8,'row'=4] {'row'}, dimensions={0}, use_global_device_ids=true | all-gather | bytes 655360 | tf_op jit(solution)/shard_map/all_gather | solution.py:11
  210.0 10.1 %while.12 = (s32[]{:T(128)}, f32[64,64]{1,0:T(8,128)}, f32[64,512]{1,0:T(8,128)S(1)}, s32[]{:T(128)}, f32[4,64,64]{2,1,0:T(8,128)}, /*index=5*/f32[4,64,512]{2,1,0:T(8,128)S(1)}, s32[]{:T(128)}, s32[]{:T(128)}, s32[]{:T(128)}) while((s32[]{:T(128)}, f32[64,64]{1,0:T(8,128)}, f32[64,512]{1,0:T(8,128)S(1)}, s32[]{:T(128)}, ...), condition=%wide.region_5.6_spmd, body=%wide.region_4.5_spmd.sunk | while | flops 28344324 | bytes 787595 | solution.py:19
  210.7 1.5 fusion.91
  217.5 1.5 fusion.91
  221.3 3.6 %fusion.10 = f32[1024,512]{0,1:T(8,128)S(1)} fusion(f32[2,1024,512]{1,2,0:T(8,128)} %bitcast.161, f32[64,512]{1,0:T(8,128)S(1)} %convolution_add_fusion.1, f32[2,1024,64]{1,2,0:T(8,128)S(1)} %fusion.42), kind=kOutput, calls=%fused_computation.14 | convolution fusion | flops 403177472 | bytes 4587520 | tf_op jit(solution)/shard_map/dot_general | solution.py:117
  226.1 1.9 fusion.9
  231.1 3.9 %copy.27 = bf16[2,1024,512]{2,1,0:T(8,128)(2,1)} copy(bf16[2,1024,512]{1,2,0:T(8,128)(2,1)} %pad_maximum_fusion) | data formatting | bytes 4194304
  (71 shorter events, 25.1 us)
Async XLA Ops:
  7.2 5.1 %copy-start = (bf16[1024,1024]{1,0:T(8,128)(2,1)S(1)}, bf16[1024,1024]{1,0:T(8,128)(2,1)}, u32[]{:S(2)}) copy-start(bf16[1024,1024]{1,0:T(8,128)(2,1)} %param.23) | copy-start | bytes 6291460
  7.2 76.8 %all-reduce.3.cloned.1.call-start = ((), (), s32[]{:S(2)}) async-start(), calls=%async_computation | async-start | bytes 1048576 | tf_op jit(solution)/shard_map/psum | solution.py:63
  12.2 173.0 %all-reduce.5.cloned.1.call-start = ((), (), s32[]{:S(2)}) async-start(), calls=%async_computation.1 | async-start | bytes 1048576 | tf_op jit(solution)/shard_map/psum | solution.py:72
  14.7 1.3 copy-start.10
  14.7 2.6 %copy-start.11 = (bf16[2,1024,64]{1,2,0:T(8,128)(2,1)S(1)}, bf16[2,1024,64]{1,2,0:T(8,128)(2,1)}, u32[]{:S(2)}) copy-start(bf16[2,1024,64]{1,2,0:T(8,128)(2,1)} %param.22) | copy-start | bytes 786436
  14.7 4.6 %copy-start.4 = (bf16[2,1024,1024]{2,1,0:T(8,128)(2,1)S(1)}, bf16[2,1024,1024]{2,1,0:T(8,128)(2,1)}, u32[]{:S(2)}) copy-start(bf16[2,1024,1024]{2,1,0:T(8,128)(2,1)} %param.24) | copy-start | bytes 12582916
  16.0 1.3 copy-start.1
  17.4 2.0 copy-start.12
  19.4 88.4 %copy-start.8 = (f32[64,64]{1,0:T(8,128)}, f32[64,64]{1,0:T(8,128)S(1)}, u32[]{:S(2)}) copy-start(f32[64,64]{1,0:T(8,128)S(1)} %fusion.33) | copy-start | bytes 49156
  85.8 27.5 %copy-start.6 = (bf16[2,1024,64]{1,2,0:T(8,128)(2,1)S(1)}, bf16[2,1024,64]{1,2,0:T(8,128)(2,1)}, u32[]{:S(2)}) copy-start(bf16[2,1024,64]{1,2,0:T(8,128)(2,1)} %param.26) | copy-start | bytes 786436
  189.2 3.6 %copy-start.7 = (f32[512,2,64]{2,1,0:T(2,128)S(1)}, f32[512,2,64]{2,1,0:T(2,128)}, u32[]{:S(2)}) copy-start(f32[512,2,64]{2,1,0:T(2,128)} %copy.28) | copy-start | bytes 786436
  189.2 3.6 %copy-start.9 = (bf16[2,1024,512]{2,1,0:T(8,128)(2,1)S(1)}, bf16[2,1024,512]{2,1,0:T(8,128)(2,1)}, u32[]{:S(2)}) copy-start(bf16[2,1024,512]{2,1,0:T(8,128)(2,1)} %param.28) | copy-start | bytes 6291460
  189.2 3.6 %copy-start.13 = (bf16[2,1024,64]{1,2,0:T(8,128)(2,1)S(1)}, bf16[2,1024,64]{1,2,0:T(8,128)(2,1)}, u32[]{:S(2)}) copy-start(bf16[2,1024,64]{1,2,0:T(8,128)(2,1)} %param.21) | copy-start | bytes 786436
  192.8 2.3 copy-start.5
  198.0 2.5 %copy-start.2 = (f32[2,512,1024]{2,1,0:T(8,128)}, f32[2,512,1024]{2,1,0:T(8,128)S(1)}, u32[]{:S(2)}) copy-start(f32[2,512,1024]{2,1,0:T(8,128)S(1)} %fusion.41) | copy-start | bytes 12582916
  221.2 4.9 %copy-start.3 = (f32[2,512,1024]{2,1,0:T(8,128)S(1)}, f32[2,512,1024]{2,1,0:T(8,128)}, u32[]{:S(2)}) copy-start(f32[2,512,1024]{2,1,0:T(8,128)} %copy-done.2) | copy-start | bytes 12582916
Sparse Core Ops, SparseCore 0:
  12.3 71.6 all-reduce.2
  113.4 71.6 all-reduce.4
where the time goes:
time: 245 us; the launch traced here: 244 us
  waiting for transfers between devices  124 us (51%)
  matrix products  52.7 us (22%)
  other arithmetic  24.4 us (10%)
  blocking collectives  17.2 us (7%)
  between operations  14.5 us (6%)
  local copies, waits for them, and re-layouts  11.1 us (5%)
    psum x1, waiting for transfers between devices, shards(): sketched = lax.psum(sketch_terms, 'col')  63.2 us
    psum x1, waiting for transfers between devices, shards(): schur_full = lax.psum(schur_terms, 'col')  60.7 us
    all_gather x2, blocking collectives, prefix(): gathered = jax.tree.map(lambda a: lax.all_gather(a, axis), part)  17.2 us
    another operation x4, other arithmetic, lower_inverse(): gram_lower = jnp.linalg.cholesky(gram_matrix)  11.9 us
    another operation x3, other arithmetic, lower_inverse(): lax.linalg.triangular_solve(gram_lower, identity_matrix, left_side=True,...  9.92 us
    dot_general x2, matrix products, shards(): jnp.dot(feed_columns[position], prior_state, precision=HIGHEST_PRECISION)  5.49 us
    unnamed x29, local copies, waits for them, and re-layouts  5.34 us
  transfers between devices with their start and end apart: 2, of which 2 were waited for; matrix products, arithmetic and copies ran while one was open for 4% of the time, Pallas kernels for 0%

commit v1 on v0

v1 whole, which is shorter than its diff:
```python
import functools

import jax
import jax.numpy as jnp
from jax import lax
from jax.experimental import pallas as pl
from jax.experimental.pallas import tpu as pltpu
from jax.sharding import PartitionSpec as P

F32 = jnp.float32
BF16 = jnp.bfloat16
LANES = 128
BLOCK = 256
NN = ((1,), (0,))
NT = ((1,), (1,))
TN = ((0,), (0,))


def halves(x):
    high = x.astype(BF16)
    return high, (x - high.astype(F32)).astype(BF16)


def bdot(a, b, dims=NN):
    return lax.dot_general(a, b, (dims, ((), ())), preferred_element_type=F32)


def dot2(a, b, dims=NN):
    high, low = halves(b)
    return bdot(a, high, dims) + bdot(a, low, dims)


def dot3(a, b, dims=NN):
    ah, al = halves(a)
    bh, bl = halves(b)
    return bdot(ah, bh, dims) + (bdot(ah, bl, dims) + bdot(al, bh, dims))


def vmem_call(body, outs, scratch=(), flops=10**7, name=None, limit=16):
    return pl.pallas_call(
        body,
        out_shape=[jax.ShapeDtypeStruct(s, d) for s, d in outs],
        scratch_shapes=list(scratch),
        compiler_params=pltpu.CompilerParams(vmem_limit_bytes=limit * 2**20),
        cost_estimate=pl.CostEstimate(flops=flops, bytes_accessed=10**6, transcendentals=0),
        name=name,
    )


def blocks_of(extent):
    size = min(BLOCK, extent)
    return [(start, start + size) for start in range(0, extent, size)]


def couple_body(tl, tr, rl, rr, sk, x_own, msg):
    parity = lax.rem(lax.axis_index("col"), 2)
    rank, nb = rl.shape

    def crossed(band):
        coupling = bdot(tr[band], rr[...], NT)
        high, low = halves(coupling)
        both = bdot(jnp.concatenate([high, low], 1), tl[band], TN)
        return both[:rank] + both[rank:]

    x_own[...] = crossed(parity)
    msg[:, :nb] = crossed(1 - parity)
    probe = bdot(rl[...], sk[...], NT)
    msg[:, nb:] = jnp.concatenate([probe, jnp.zeros_like(probe)], 1)


def sketch_body(pieces, x_own, sent, got, x_pair, *rest):
    outs, part = rest[:-1], rest[-1]
    col = lax.axis_index("col")
    parity = lax.rem(col, 2)
    place = col // 2
    rank, nb = x_own.shape
    own, other = x_own[...], got[:, :nb]
    probes = jnp.concatenate([sent[:, nb : nb + rank], got[:, nb : nb + rank]], 0)
    part[...] = dot3(probes, jnp.concatenate([own, other], 0), TN)
    x_pair[pl.ds(pl.multiple_of(parity * rank, rank), rank), :] = own
    x_pair[pl.ds(pl.multiple_of((1 - parity) * rank, rank), rank), :] = other
    slab = nb // pieces
    for step in range(pieces):
        start = pl.multiple_of(jnp.bitwise_xor(place, step) * slab, slab) if pieces > 1 else 0
        outs[step][...] = part[:, pl.ds(start, slab)]


def project_body(pieces, x_pair, *rest):
    slabs, (sk, crossed, gram) = rest[:pieces], rest[pieces:]
    place = lax.axis_index("col") // 2
    slab = slabs[0].shape[1]
    for step in range(pieces):
        start = pl.multiple_of(jnp.bitwise_xor(place, step) * slab, slab) if pieces > 1 else 0
        sk[:, pl.ds(start, slab)] = slabs[step][...]
    whole = sk[...]
    crossed[...] = dot3(whole, x_pair[...], NT)
    gram[...] = lax.dot_general(
        whole, whole, (NT, ((), ())), precision=lax.Precision.HIGHEST, preferred_element_type=F32
    )


def widen_body(row_left, out):
    half = out.shape[1]
    start = pl.multiple_of(lax.rem(lax.axis_index("row"), 2) * half, half)
    out[...] = row_left[:, pl.ds(start, half)].astype(F32)


def narrow_body(groups, *refs):
    blocks, out = refs[:-1], refs[-1]
    half = blocks[0].shape[-1]
    parity = lax.rem(lax.axis_index("col"), 2)
    near_start = pl.multiple_of(lax.rem(lax.axis_index("row"), 2) * half, half)
    far_start = pl.multiple_of(half - near_start, half)
    index = 0
    for start in (near_start, far_start):
        for side in (parity, 1 - parity):
            for step in range(groups):
                out[step, side, :, pl.ds(start, half)] = blocks[index][...].astype(BF16)
                index += 1


def wide_pulled_body(wide, pulled, high_out, low_out):
    pulled_high, pulled_low = halves(pulled[...])
    for first, last in blocks_of(wide.shape[0]):
        rows = wide[first:last, :]
        product = bdot(rows, pulled_high) + bdot(rows, pulled_low)
        high, low = halves(product)
        high_out[first:last, :] = high
        low_out[first:last, :] = low


def factor_body(gram, out):
    rank = gram.shape[0]
    lanes = 2 * rank
    group = 4
    tile = 8
    rows = lax.broadcasted_iota(jnp.int32, (rank, lanes), 0)
    cols = lax.broadcasted_iota(jnp.int32, (rank, lanes), 1)
    eye = jnp.where(cols == rows + rank, 1.0, 0.0).astype(F32)
    work = jnp.concatenate([gram[...], jnp.zeros((rank, rank), F32)], 1) + eye
    done = []
    scales = []
    for start in range(0, rank, group):
        top = (start // tile) * tile
        if start == top and start:
            done.append(work[:tile])
            work = work[tile:]
        ids = rows[top:]
        height = rank - top
        columns = [
            jnp.broadcast_to(work[:, start + j : start + j + 1], (height, lanes)) for j in range(group)
        ]
        for j in range(group):
            k = start + j
            at = k - top
            pivot = columns[j][at : at + 1, :]
            inverse = 1.0 / pivot
            scales.append(lax.rsqrt(pivot))
            factor = jnp.where(ids > k, columns[j] * inverse, 0.0)
            for later in range(j + 1, group):
                columns[later] = columns[later] - factor * columns[later][at : at + 1, :]
            work = work - factor * work[at : at + 1, :]
    done.append(work)
    whole = jnp.concatenate(done, 0) * jnp.concatenate(scales, 0)
    out[...] = whole[:, rank:]


def scaled_body(groups, inverse, *rest):
    blocks, out = rest[:groups], rest[groups]
    low = inverse[...]
    width = blocks[0].shape[1]
    for step in range(groups):
        out[:, step * width : (step + 1) * width] = dot3(low, blocks[step][...])
    out[:, groups * width :] = jnp.concatenate([low, jnp.zeros_like(low)], 1)


def band_body(pr, pl_t, ll, right, pulled, inverse, rhs, base, feed, offset, gain, right_rows, red):
    rank, nb = right.shape
    coeffs = dot2(pr[...], pulled[...])
    coeffs_two = jnp.concatenate(halves(coeffs), 0)
    left = pl_t[...]
    left_two = jnp.concatenate([left, left], 0)
    for first, last in blocks_of(nb):
        term = bdot(left_two[:, first:last], coeffs_two, TN)
        red[first:last, :] = (rhs[first:last, :].astype(F32) - term).astype(BF16)
    for first, last in blocks_of(nb):
        rows = inverse[first:last, :last]
        base[first:last, :] = bdot(rows, red[:last, :])
        feed_high, feed_low = halves(bdot(rows, ll[:, :last], NT))
        feed[first:last, :] = jnp.concatenate([feed_high, feed_high, feed_low], 1)
        right_rows[:, first:last] = bdot(right[:, first:], inverse[first:, first:last])
    two = jnp.concatenate(halves(right_rows[...]), 0)
    both = bdot(two, red[...])
    offset[...] = both[:rank] + both[rank:]
    both = bdot(two, ll[...], NT)
    gain[...] = both[:rank] + both[rank:]


def spread_body(inverse, right_rows, own, other, spread, spread_gain):
    parity = lax.rem(lax.axis_index("col"), 2)
    rank, nb = own.shape
    for side, sk in ((parity, own), (1 - parity, other)):
        two = jnp.concatenate(halves(sk[...]), 0)
        for first, last in blocks_of(nb):
            both = bdot(inverse[side, first:last, :last], two[:, :last], NT)
            high, low = halves(both[:, :rank] + both[:, rank:])
            spread[side, first:last, :] = jnp.concatenate([high, high, low], 1)
        spread_gain[side] = dot3(right_rows[side], sk[...], NT)


def stack3(x):
    high, low = halves(x)
    return jnp.concatenate([high, low, high], 0)


def weight_body(own, other, wp_high, wp_low, offset, gain, spread_gain, weights, offsets, pack):
    parity = lax.rem(lax.axis_index("col"), 2)
    rank = gain.shape[1]
    count = wp_high.shape[0]
    width = wp_high.shape[1]
    for side, middle in ((parity, own), (1 - parity, other)):
        mixed = dot3(middle[:, count : count + rank], middle[:, :count], TN)
        high, low = halves(mixed)
        both = bdot(jnp.concatenate([high, low], 0), wp_high[...])
        weight = both[:rank] + (both[rank:] + bdot(high, wp_low[...]))
        weights[side] = stack3(weight)
        offsets[side] = offset[side] + dot3(spread_gain[side], weight)
    map_offset = offsets[0]
    map_matrix = -gain[0]
    for band in range(1, gain.shape[0]):
        map_offset = offsets[band] - dot3(gain[band], map_offset)
        map_matrix = -dot3(gain[band], map_matrix)
    pack[:, :width] = map_offset
    pack[:, width:] = jnp.concatenate([map_matrix, jnp.zeros_like(map_matrix)], 1)


def compose_body(bit, first, width, near, group, other, near_out, group_out):
    rank = group.shape[0]
    upper = lax.rem(lax.axis_index("row") // bit, 2) == 1

    def chained(then, before):
        matrix = then[:, width : width + rank]
        moved = dot3(matrix, before)
        lanes = lax.broadcasted_iota(jnp.int32, moved.shape, 1)
        return moved + jnp.where(lanes < width, then, 0.0)

    own, far = group[...], other[...]
    group_out[...] = chained(jnp.where(upper, own, far), jnp.where(upper, far, own))
    if first:
        lanes = lax.broadcasted_iota(jnp.int32, own.shape, 1)
        rows = lax.broadcasted_iota(jnp.int32, own.shape, 0)
        identity = jnp.where(lanes == rows + width, 1.0, 0.0).astype(F32)
        near_out[...] = jnp.where(upper, far, identity)
    else:
        near_out[...] = jnp.where(upper, chained(near[...], far), near[...])


def partial_body(base, spread, weights, middle_own, middle_other, slab, out, schur):
    parity = lax.rem(lax.axis_index("col"), 2)
    bands, nb, _ = base.shape
    rank = schur.shape[1]
    count = slab.shape[0]
    for band in range(bands):
        for first, last in blocks_of(nb):
            out[band, first:last, :] = base[band, first:last, :] + bdot(
                spread[band, first:last, :], weights[band]
            )
    for side, middle in ((parity, middle_own), (1 - parity, middle_other)):
        both = bdot(jnp.concatenate(halves(middle[:, :count]), 0), slab[...])
        schur[side] = both[:rank] + both[rank:]


def finish_body(bit, partial, feed, gain, offsets, near, other, carry, solved, states):
    bands, nb, width = partial.shape
    rank = gain.shape[1]
    upper = lax.rem(lax.axis_index("row") // bit, 2) == 1
    prior = carry[...]
    far = dot3(other[:, width : width + rank], prior) + other[:, :width]
    prior = jnp.where(upper, far, prior)
    prior = dot3(near[:, width : width + rank], prior) + near[:, :width]
    for band in range(bands):
        three = stack3(prior)
        prior = offsets[band] - dot3(gain[band], prior)
        states[band] = prior
        for first, last in blocks_of(nb):
            solved[band, first:last, :] = (
                partial[band, first:last, :] - bdot(feed[band, first:last, :], three)
            ).astype(BF16)


def shards(
    tile_left,
    tile_right,
    row_left,
    row_right,
    sketch,
    panel_left,
    panel_right,
    pivot_inverse,
    band_inverse,
    link_left,
    link_right,
    pivot_rhs,
    band_rhs,
    carry_in,
):
    cols = lax.axis_size("col")
    rows = lax.axis_size("row")
    groups = cols // 2
    col = lax.axis_index("col")
    bands, nb, rank = tile_left.shape[1:]
    width = pivot_rhs.shape[1]
    slab = nb // groups
    count = cols * rank

    def swap(x, step):
        return lax.ppermute(x, "col", [(c, c ^ step) for c in range(cols)])

    def row_swap(x, step):
        return lax.ppermute(x, "row", [(r, r ^ step) for r in range(rows)])

    def turned(x):
        return jnp.swapaxes(x, -1, -2)

    row_left_t = turned(row_left[0])
    x_own, x_sent = vmem_call(
        couple_body, [((rank, nb), F32), ((rank, nb + LANES), F32)], name="couple"
    )(turned(tile_left[0]), turned(tile_right[0]), row_left_t, turned(row_right[0]), turned(sketch))
    x_got = swap(x_sent, 1)

    wide = list(vmem_call(widen_body, [((rank, nb // 2), F32)], name="widen")(row_left_t))
    step = 1
    while step < groups:
        wide = wide + [swap(block, 2 * step) for block in wide]
        step *= 2
    wide = wide + [swap(block, 1) for block in wide]
    wide = wide + [row_swap(block, 1) for block in wide]
    (wide,) = vmem_call(
        functools.partial(narrow_body, groups), [((groups, 2, rank, nb), BF16)], name="narrow"
    )(*wide)
    wide = wide.reshape(count, nb)

    pivot_solution = jnp.dot(pivot_inverse, pivot_rhs, preferred_element_type=F32).astype(BF16)
    pulled = bdot(pivot_inverse, pivot_solution, TN)

    def per_band(*shape):
        return pl.BlockSpec((None,) + shape, lambda band: (band, 0, 0))

    base, feed, offset, gain, right_rows = pl.pallas_call(
        band_body,
        grid=(bands,),
        in_specs=[per_band(rank, nb)] * 4
        + [pl.BlockSpec((nb, width), lambda band: (0, 0)), per_band(nb, nb), per_band(nb, width)],
        out_specs=[
            per_band(nb, width),
            per_band(nb, 3 * rank),
            per_band(rank, width),
            per_band(rank, rank),
            per_band(rank, nb),
        ],
        out_shape=[
            jax.ShapeDtypeStruct((bands, nb, width), F32),
            jax.ShapeDtypeStruct((bands, nb, 3 * rank), BF16),
            jax.ShapeDtypeStruct((bands, rank, width), F32),
            jax.ShapeDtypeStruct((bands, rank, rank), F32),
            jax.ShapeDtypeStruct((bands, rank, nb), F32),
        ],
        scratch_shapes=[pltpu.VMEM((nb, width), BF16)],
        compiler_params=pltpu.CompilerParams(vmem_limit_bytes=32 * 2**20),
        cost_estimate=pl.CostEstimate(flops=4 * 10**9, bytes_accessed=10**7, transcendentals=0),
        name="band",
    )(
        turned(panel_right),
        turned(panel_left),
        turned(link_left),
        turned(link_right),
        pulled,
        band_inverse,
        band_rhs,
    )

    pieces = groups if slab % LANES == 0 else 1
    parts = vmem_call(
        functools.partial(sketch_body, pieces),
        [((2 * rank, nb), F32)] + [((rank, nb // pieces), F32)] * pieces,
        [pltpu.VMEM((rank, nb), F32)],
        name="sketch",
    )(x_own, x_sent, x_got)
    x_pair, parts = parts[0], parts[1:]
    if pieces > 1:
        total = parts[0]
        for step in range(1, pieces):
            total = total + swap(parts[step], 2 * step)
        slabs = [total] + [swap(total, 2 * step) for step in range(1, pieces)]
    else:
        members = [list(range(side, cols, 2)) for side in range(2)]
        slabs = [lax.psum(parts[0], "col", axis_index_groups=members)]
    sketched, crossed, gram = vmem_call(
        functools.partial(project_body, pieces),
        [((rank, nb), F32), ((rank, 2 * rank), F32), ((rank, rank), F32)],
        name="project",
    )(x_pair, *slabs)
    crossed_all = [crossed] + [swap(crossed, 2 * step) for step in range(1, groups)]
    sketched_other = swap(sketched, 1)
    (inverse_low,) = vmem_call(factor_body, [((rank, rank), F32)], name="factor")(gram)
    (middle,) = vmem_call(
        functools.partial(scaled_body, groups), [((rank, count + LANES), F32)], name="scaled"
    )(inverse_low, *crossed_all)
    middle_other = swap(middle, 1)

    wp_high, wp_low = vmem_call(
        wide_pulled_body,
        [((count, width), BF16)] * 2,
        flops=10**9,
        name="wide_pulled",
        limit=32,
    )(wide, pulled)
    spread, spread_gain = vmem_call(
        spread_body,
        [((bands, nb, 3 * rank), BF16), ((bands, rank, rank), F32)],
        flops=10**9,
        name="spread",
        limit=32,
    )(band_inverse, right_rows, sketched, sketched_other)
    weights, offsets, pack = vmem_call(
        weight_body,
        [
            ((bands, 3 * rank, width), BF16),
            ((bands, rank, width), F32),
            ((rank, width + LANES), F32),
        ],
        name="weight",
        limit=32,
    )(middle, middle_other, wp_high, wp_low, offset, gain, spread_gain)

    near, group = pack, pack
    step = 1
    while step < rows:
        other = row_swap(group, step)
        if 2 * step < rows:
            near, group = vmem_call(
                functools.partial(compose_body, step, step == 1, width),
                [((rank, width + LANES), F32)] * 2,
                name="compose",
            )(near, group, other)
        step *= 2

    own_slab = lax.dynamic_slice_in_dim(wide, col * (nb // cols), nb // cols, 1)
    partial, schur = vmem_call(
        partial_body,
        [((bands, nb, width), F32), ((bands, rank, nb // cols), F32)],
        flops=10**9,
        name="partial",
        limit=32,
    )(base, spread, weights, middle, middle_other, own_slab)
    solved, states = vmem_call(
        functools.partial(finish_body, rows // 2),
        [((bands, nb, width), BF16), ((bands, rank, width), F32)],
        flops=10**9,
        name="finish",
        limit=32,
    )(partial, feed, gain, offsets, near, other, carry_in)
    return (pivot_solution, turned(schur), solved, states)


def solution(mesh):
    return jax.shard_map(
        shards,
        mesh=mesh,
        in_specs=(
            P("col", "row", None, None),
            P("col", "row", None, None),
            P("col", None, None),
            P("col", None, None),
            P(),
            P("row", None, None),
            P("row", None, None),
            P(),
            P("row", None, None),
            P("row", None, None),
            P("row", None, None),
            P(None, "col"),
            P("row", None, "col"),
            P(None, "col"),
        ),
        out_specs=(
            P(None, "col"),
            P("row", "col", None),
            P("row", None, "col"),
            P("row", None, "col"),
        ),
        check_vma=False,
    )
```

time: 245 us -> 90.1 us (0.37)
  the two profiles are of different devices: /device:TPU:3 before, /device:TPU:0 now
where the time goes in v1:
time: 90.1 us; the launch traced here: 89.7 us
  starting transfers between devices  30.4 us (34%)
  waiting for transfers between devices  21.5 us (24%)
  Pallas kernels  19.8 us (22%)
  local copies, waits for them, and re-layouts  14.6 us (16%)
  matrix products  2.54 us (3%)
  between operations  0.92 us (1%)
    ppermute x19, starting transfers between devices, swap(): return lax.ppermute(x, 'col', [(c, c ^ step) for c in range(cols)])  27.7 us
    ppermute x19, waiting for transfers between devices, swap(): return lax.ppermute(x, 'col', [(c, c ^ step) for c in range(cols)])  19.8 us
    unnamed x52, local copies, waits for them, and re-layouts  14.5 us
    pallas_call x1, Pallas kernels, shards(): pl.pallas_call(band_body, grid=(bands,), in_specs=[per_band(rank, nb)] *...  5.08 us
    pallas_call x1, Pallas kernels, shards(): vmem_call(factor_body, [((rank, rank), F32)], name='factor')(gram)  2.74 us
    ppermute x10, starting transfers between devices, row_swap(): return lax.ppermute(x, 'row', [(r, r ^ step) for r in range(rows)])  2.69 us
    pallas_call x1, Pallas kernels, shards(): vmem_call(functools.partial(finish_body, rows // 2), [((bands, nb, width)...  2.52 us
    pallas_call x1, Pallas kernels, shards(): vmem_call(weight_body, [((bands, 3 * rank, width), BF16), ((bands, rank,...  2.04 us
  transfers between devices with their start and end apart: 29, of which 8 were waited for; matrix products, arithmetic and copies ran while one was open for 3% of the time, Pallas kernels for 14%

profile of v1, /device:TPU:0, one launch (start us, length us, event | category | flops | bytes accessed | tf_op | source)
XLA Modules:
  0.0 89.7 jit_solution(38494171568549998)
XLA Ops:
  6.3 3.0 %collective-permute-start = (f32[64,1152]{1,0:T(8,128)S(1)}, f32[64,1152]{1,0:T(8,128)S(1)}, u32[]{:S(2)}, u32[]{:S(2)}) collective-permute-start(f32[64,1152]{1,0:T(8,128)S(1)} %get-tuple-element.35.sent), channel_id=1, source_target_pairs={{0,4},{4,0},{8,12},{12,8},{16,20},{20,16},{24,28},{28,24},{1,5},{5... | collective-permute-start | bytes 884744 | tf_op jit(solution)/shard_map/ppermute | solution.py:317
  9.4 7.0 %collective-permute-done.got = f32[64,1152]{1,0:T(8,128)S(1)} collective-permute-done((f32[64,1152]{1,0:T(8,128)S(1)}, f32[64,1152]{1,0:T(8,128)S(1)}, u32[]{:S(2)}, u32[]{:S(2)}) %collective-permute-start) | collective-permute-done | bytes 294944 | tf_op jit(solution)/shard_map/ppermute | solution.py:317
  16.8 1.9 %collective-permute-start.1 = (f32[64,256]{1,0:T(8,128)S(1)}, f32[64,256]{1,0:T(8,128)S(1)}, u32[]{:S(2)}, u32[]{:S(2)}) collective-permute-start(f32[64,256]{1,0:T(8,128)S(1)} %get-tuple-element.38), channel_id=1, source_target_pairs={{0,8},{4,12},{8,0},{12,4},{16,24},{20,28},{24,16},{28,20},{1,9},{5... | collective-permute-start | bytes 196616 | tf_op jit(solution)/shard_map/ppermute | solution.py:317
  18.6 2.6 %collective-permute-start.2 = (f32[64,256]{1,0:T(8,128)S(1)}, f32[64,256]{1,0:T(8,128)S(1)}, u32[]{:S(2)}, u32[]{:S(2)}) collective-permute-start(f32[64,256]{1,0:T(8,128)S(1)} %get-tuple-element.39), channel_id=1, source_target_pairs={{0,16},{4,20},{8,24},{12,28},{16,0},{20,4},{24,8},{28,12},{1,17},{... | collective-permute-start | bytes 196616 | tf_op jit(solution)/shard_map/ppermute | solution.py:317
  22.2 1.8 %collective-permute-start.15 = (f32[64,512]{1,0:T(8,128)S(1)}, f32[64,512]{1,0:T(8,128)S(1)}, u32[]{:S(2)}, u32[]{:S(2)}) collective-permute-start(f32[64,512]{1,0:T(8,128)S(1)} %widen.1.refs_0_), channel_id=1, source_target_pairs={{0,4},{4,0},{8,12},{12,8},{16,20},{20,16},{24,28},{28,24},{1,5},{5... | collective-permute-start | bytes 393224 | tf_op jit(solution)/shard_map/ppermute | solution.py:317
  24.0 1.7 %collective-permute-start.13 = (f32[64,512]{1,0:T(8,128)S(1)}, f32[64,512]{1,0:T(8,128)S(1)}, u32[]{:S(2)}, u32[]{:S(2)}) collective-permute-start(f32[64,512]{1,0:T(8,128)S(1)} %widen.1.refs_0_), channel_id=1, source_target_pairs={{0,16},{4,20},{8,24},{12,28},{16,0},{20,4},{24,8},{28,12},{1,17},{... | collective-permute-start | bytes 393224 | tf_op jit(solution)/shard_map/ppermute | solution.py:317
  25.7 2.5 %collective-permute-start.12 = (f32[64,512]{1,0:T(8,128)S(1)}, f32[64,512]{1,0:T(8,128)S(1)}, u32[]{:S(2)}, u32[]{:S(2)}) collective-permute-start(f32[64,512]{1,0:T(8,128)S(1)} %widen.1.refs_0_), channel_id=1, source_target_pairs={{0,8},{4,12},{8,0},{12,4},{16,24},{20,28},{24,16},{28,20},{1,9},{5... | collective-permute-start | bytes 393224 | tf_op jit(solution)/shard_map/ppermute | solution.py:317
  29.8 2.9 %collective-permute-start.4 = (f32[64,256]{1,0:T(8,128)S(1)}, f32[64,256]{1,0:T(8,128)S(1)}, u32[]{:S(2)}, u32[]{:S(2)}) collective-permute-start(f32[64,256]{1,0:T(8,128)S(1)} %add_add_fusion.rest_0_), channel_id=1, source_target_pairs={{0,8},{4,12},{8,0},{12,4},{16,24},{20,28},{24,16},{28,20},{1,9},{5... | collective-permute-start | bytes 196616 | tf_op jit(solution)/shard_map/ppermute | solution.py:317
  32.7 1.6 %collective-permute-done.13.refs_2_ = f32[64,512]{1,0:T(8,128)S(1)} collective-permute-done((f32[64,512]{1,0:T(8,128)S(1)}, f32[64,512]{1,0:T(8,128)S(1)}, u32[]{:S(2)}, u32[]{:S(2)}) %collective-permute-start.13) | collective-permute-done | bytes 131104 | tf_op jit(solution)/shard_map/ppermute | solution.py:317
  36.3 2.7 %collective-permute-done.5.rest_2_ = f32[64,256]{1,0:T(8,128)S(1)} collective-permute-done((f32[64,256]{1,0:T(8,128)S(1)}, f32[64,256]{1,0:T(8,128)S(1)}, u32[]{:S(2)}, u32[]{:S(2)}) %collective-permute-start.5) | collective-permute-done | bytes 65568 | tf_op jit(solution)/shard_map/ppermute | solution.py:317
  42.1 5.0 %collective-permute-done.14.refs_3_ = f32[64,512]{1,0:T(8,128)S(1)} collective-permute-done((f32[64,512]{1,0:T(8,128)S(1)}, f32[64,512]{1,0:T(8,128)S(1)}, u32[]{:S(2)}, u32[]{:S(2)}) %collective-permute-start.14) | collective-permute-done | bytes 131104 | tf_op jit(solution)/shard_map/ppermute | solution.py:317
  47.1 1.5 %collective-permute-start.18 = (f32[64,512]{1,0:T(8,128)S(1)}, f32[64,512]{1,0:T(8,128)S(1)}, u32[]{:S(2)}, u32[]{:S(2)}) collective-permute-start(f32[64,512]{1,0:T(8,128)S(1)} %collective-permute-done.14.refs_3_), channel_id=1, source_target_pairs={{0,4},{4,0},{8,12},{12,8},{16,20},{20,16},{24,28},{28,24},{1,5},{5... | collective-permute-start | bytes 393224 | tf_op jit(solution)/shard_map/ppermute | solution.py:317
  48.6 1.8 %collective-permute-start.10 = (f32[64,128]{1,0:T(8,128)S(1)}, f32[64,128]{1,0:T(8,128)S(1)}, u32[]{:S(2)}, u32[]{:S(2)}) collective-permute-start(f32[64,128]{1,0:T(8,128)S(1)} %get-tuple-element.44.rest_0_), channel_id=1, source_target_pairs={{0,24},{4,28},{8,16},{12,20},{16,8},{20,12},{24,0},{28,4},{1,25},{... | collective-permute-start | bytes 98312 | tf_op jit(solution)/shard_map/ppermute | solution.py:317
  50.5 2.6 %collective-permute-start.8 = (f32[64,128]{1,0:T(8,128)S(1)}, f32[64,128]{1,0:T(8,128)S(1)}, u32[]{:S(2)}, u32[]{:S(2)}) collective-permute-start(f32[64,128]{1,0:T(8,128)S(1)} %get-tuple-element.44.rest_0_), channel_id=1, source_target_pairs={{0,8},{4,12},{8,0},{12,4},{16,24},{20,28},{24,16},{28,20},{1,9},{5... | collective-permute-start | bytes 98312 | tf_op jit(solution)/shard_map/ppermute | solution.py:317
  56.8 5.1 %band.1 = (f32[2,1024,512]{2,1,0:T(8,128)S(1)}, bf16[2,1024,192]{2,1,0:T(8,128)(2,1)S(1)}, f32[2,64,512]{2,1,0:T(8,128)S(1)}, f32[2,64,64]{2,1,0:T(8,128)S(1)}, f32[2,64,1024]{2,1,0:T(8,128)S(1)}) custom-call(bf16[2,64,1024]{2,1,0:T(8,128)(2,1)S(1)} %bitcast.33, bf16[2,64,1024]{2,1,0:T(8,128)(2,1)S(1)} %bitcast.34, bf16[2,64,1024]{2,1,0:T(8,128)(2,1)S(1)} %bitcast.35, ...), custom_call_target="tpu_custom_call" | custom-call | flops 4000000000 | bytes 10000000 | tf_op jit(solution)/shard_map/band/pallas_call | solution.py:349
  61.9 2.0 %copy-done.2 = f32[2,1024,512]{2,1,0:T(8,128)} copy-done((f32[2,1024,512]{2,1,0:T(8,128)}, f32[2,1024,512]{2,1,0:T(8,128)S(1)}, u32[]{:S(2)}) %copy-start.2) | copy-done | bytes 4194328
  63.9 2.7 %factor.1.inverse = f32[64,64]{1,0:T(8,128)S(1)} custom-call(f32[64,64]{1,0:T(8,128)S(1)} %get-tuple-element.43.gram), custom_call_target="tpu_custom_call" | custom-call | flops 10000000 | bytes 1000000 | tf_op jit(solution)/shard_map/factor/pallas_call | solution.py:405
  71.2 2.0 %collective-permute-done.11.other.middle_other = f32[64,640]{1,0:T(8,128)S(1)} collective-permute-done((f32[64,640]{1,0:T(8,128)S(1)}, f32[64,640]{1,0:T(8,128)S(1)}, u32[]{:S(2)}, u32[]{:S(2)}) %collective-permute-start.11) | collective-permute-done | bytes 163872 | tf_op jit(solution)/shard_map/ppermute | solution.py:317
  73.2 2.0 %weight.1 = (bf16[2,192,512]{2,1,0:T(8,128)(2,1)S(1)}, f32[2,64,512]{2,1,0:T(8,128)S(1)}, f32[64,640]{1,0:T(8,128)}) custom-call(f32[64,640]{1,0:T(8,128)S(1)} %scaled.1.own.middle_own, f32[64,640]{1,0:T(8,128)S(1)} %collective-permute-done.11.other.middle_other, bf16[512,512]{1,0:T(8,128)(2,1)S(1)} %get-tuple-element.45.wp_high, ...), custom_call_target="tpu_custom_call" | custom-call | flops 10000000 | bytes 1000000 | tf_op jit(solution)/shard_map/weight/pallas_call | solution.py:425
  76.7 1.7 %collective-permute-done.27.other = f32[64,640]{1,0:T(8,128)} collective-permute-done((f32[64,640]{1,0:T(8,128)}, f32[64,640]{1,0:T(8,128)}, u32[]{:S(2)}, u32[]{:S(2)}) %collective-permute-start.27) | collective-permute-done | bytes 163872 | tf_op jit(solution)/shard_map/ppermute | solution.py:320
  79.8 1.6 %collective-permute-start.28 = (f32[64,640]{1,0:T(8,128)S(1)}, f32[64,640]{1,0:T(8,128)S(1)}, u32[]{:S(2)}, u32[]{:S(2)}) collective-permute-start(f32[64,640]{1,0:T(8,128)S(1)} %get-tuple-element.57), channel_id=1, source_target_pairs={{0,2},{1,3},{2,0},{3,1},{4,6},{5,7},{6,4},{7,5},{8,10},{9,11},{10,... | collective-permute-start | bytes 491528 | tf_op jit(solution)/shard_map/ppermute | solution.py:320
  81.4 2.2 %copy-done.3 = f32[2,1024,512]{2,1,0:T(8,128)S(1)} copy-done((f32[2,1024,512]{2,1,0:T(8,128)S(1)}, f32[2,1024,512]{2,1,0:T(8,128)}, u32[]{:S(2)}) %copy-start.3) | copy-done | bytes 4194328
  85.8 1.4 %partial.1 = (f32[2,1024,512]{2,1,0:T(8,128)S(1)}, f32[2,64,128]{2,1,0:T(8,128)}) custom-call(f32[2,1024,512]{2,1,0:T(8,128)S(1)} %copy-done.3, bf16[2,1024,192]{2,1,0:T(8,128)(2,1)S(1)} %copy-done.7, bf16[2,192,512]{2,1,0:T(8,128)(2,1)S(1)} %copy-done.11, f32[64,640]{1,0:T(8,128)S(1)} %scaled.1.own.middle_own, ...), custom_call_target="tpu_custom_call" | custom-call | flops 1000000000 | bytes 1000000 | tf_op jit(solution)/shard_map/partial/pallas_call | solution.py:449
  87.2 2.5 %finish.1 = (bf16[2,1024,512]{2,1,0:T(8,128)(2,1)}, f32[2,64,512]{2,1,0:T(8,128)}) custom-call(f32[2,1024,512]{2,1,0:T(8,128)S(1)} %get-tuple-element.52.partial, bf16[2,1024,192]{2,1,0:T(8,128)(2,1)S(1)} %copy-done.5, f32[2,64,64]{2,1,0:T(8,128)S(1)} %get-tuple-element.48.gain, f32[2,64,512]{2,1,0:T(8,128)S(1)} %copy-done.15, ...), custom_call_target="tpu_custom_call" | custom-call | flops 1000000000 | bytes 1000000 | tf_op jit(solution)/shard_map/finish/pallas_call | solution.py:456
  (104 shorter events, 27.0 us)
Async XLA Ops:
  6.3 10.0 %collective-permute-start = (f32[64,1152]{1,0:T(8,128)S(1)}, f32[64,1152]{1,0:T(8,128)S(1)}, u32[]{:S(2)}, u32[]{:S(2)}) collective-permute-start(f32[64,1152]{1,0:T(8,128)S(1)} %get-tuple-element.35.sent), channel_id=1, source_target_pairs={{0,4},{4,0},{8,12},{12,8},{16,20},{20,16},{24,28},{28,24},{1,5},{5... | collective-permute-start | bytes 884744 | tf_op jit(solution)/shard_map/ppermute | solution.py:317
  16.8 7.3 %collective-permute-start.1 = (f32[64,256]{1,0:T(8,128)S(1)}, f32[64,256]{1,0:T(8,128)S(1)}, u32[]{:S(2)}, u32[]{:S(2)}) collective-permute-start(f32[64,256]{1,0:T(8,128)S(1)} %get-tuple-element.38), channel_id=1, source_target_pairs={{0,8},{4,12},{8,0},{12,4},{16,24},{20,28},{24,16},{28,20},{1,9},{5... | collective-permute-start | bytes 196616 | tf_op jit(solution)/shard_map/ppermute | solution.py:317
  18.6 7.1 %collective-permute-start.2 = (f32[64,256]{1,0:T(8,128)S(1)}, f32[64,256]{1,0:T(8,128)S(1)}, u32[]{:S(2)}, u32[]{:S(2)}) collective-permute-start(f32[64,256]{1,0:T(8,128)S(1)} %get-tuple-element.39), channel_id=1, source_target_pairs={{0,16},{4,20},{8,24},{12,28},{16,0},{20,4},{24,8},{28,12},{1,17},{... | collective-permute-start | bytes 196616 | tf_op jit(solution)/shard_map/ppermute | solution.py:317
  21.2 7.0 %collective-permute-start.3 = (f32[64,256]{1,0:T(8,128)S(1)}, f32[64,256]{1,0:T(8,128)S(1)}, u32[]{:S(2)}, u32[]{:S(2)}) collective-permute-start(f32[64,256]{1,0:T(8,128)S(1)} %get-tuple-element.40), channel_id=1, source_target_pairs={{0,24},{4,28},{8,16},{12,20},{16,8},{20,12},{24,0},{28,4},{1,25},{... | collective-permute-start | bytes 196616 | tf_op jit(solution)/shard_map/ppermute | solution.py:317
  22.1 6.4 %collective-permute-start.19 = (f32[64,512]{1,0:T(8,128)S(1)}, f32[64,512]{1,0:T(8,128)S(1)}, u32[]{:S(2)}, u32[]{:S(2)}) collective-permute-start(f32[64,512]{1,0:T(8,128)S(1)} %widen.1.refs_0_), channel_id=1, source_target_pairs={{0,1},{1,0},{2,3},{3,2},{4,5},{5,4},{6,7},{7,6},{8,9},{9,8},{10,11... | collective-permute-start | bytes 393224 | tf_op jit(solution)/shard_map/ppermute | solution.py:320
  22.2 7.5 %collective-permute-start.15 = (f32[64,512]{1,0:T(8,128)S(1)}, f32[64,512]{1,0:T(8,128)S(1)}, u32[]{:S(2)}, u32[]{:S(2)}) collective-permute-start(f32[64,512]{1,0:T(8,128)S(1)} %widen.1.refs_0_), channel_id=1, source_target_pairs={{0,4},{4,0},{8,12},{12,8},{16,20},{20,16},{24,28},{28,24},{1,5},{5... | collective-permute-start | bytes 393224 | tf_op jit(solution)/shard_map/ppermute | solution.py:317
  24.0 10.3 %collective-permute-start.13 = (f32[64,512]{1,0:T(8,128)S(1)}, f32[64,512]{1,0:T(8,128)S(1)}, u32[]{:S(2)}, u32[]{:S(2)}) collective-permute-start(f32[64,512]{1,0:T(8,128)S(1)} %widen.1.refs_0_), channel_id=1, source_target_pairs={{0,16},{4,20},{8,24},{12,28},{16,0},{20,4},{24,8},{28,12},{1,17},{... | collective-permute-start | bytes 393224 | tf_op jit(solution)/shard_map/ppermute | solution.py:317
  25.7 8.6 %collective-permute-start.12 = (f32[64,512]{1,0:T(8,128)S(1)}, f32[64,512]{1,0:T(8,128)S(1)}, u32[]{:S(2)}, u32[]{:S(2)}) collective-permute-start(f32[64,512]{1,0:T(8,128)S(1)} %widen.1.refs_0_), channel_id=1, source_target_pairs={{0,8},{4,12},{8,0},{12,4},{16,24},{20,28},{24,16},{28,20},{1,9},{5... | collective-permute-start | bytes 393224 | tf_op jit(solution)/shard_map/ppermute | solution.py:317
  28.2 8.0 %collective-permute-start.6 = (f32[64,256]{1,0:T(8,128)S(1)}, f32[64,256]{1,0:T(8,128)S(1)}, u32[]{:S(2)}, u32[]{:S(2)}) collective-permute-start(f32[64,256]{1,0:T(8,128)S(1)} %add_add_fusion.rest_0_), channel_id=1, source_target_pairs={{0,24},{4,28},{8,16},{12,20},{16,8},{20,12},{24,0},{28,4},{1,25},{... | collective-permute-start | bytes 196616 | tf_op jit(solution)/shard_map/ppermute | solution.py:317
  28.5 10.4 %collective-permute-start.5 = (f32[64,256]{1,0:T(8,128)S(1)}, f32[64,256]{1,0:T(8,128)S(1)}, u32[]{:S(2)}, u32[]{:S(2)}) collective-permute-start(f32[64,256]{1,0:T(8,128)S(1)} %add_add_fusion.rest_0_), channel_id=1, source_target_pairs={{0,16},{4,20},{8,24},{12,28},{16,0},{20,4},{24,8},{28,12},{1,17},{... | collective-permute-start | bytes 196616 | tf_op jit(solution)/shard_map/ppermute | solution.py:317
  29.8 9.6 %collective-permute-start.4 = (f32[64,256]{1,0:T(8,128)S(1)}, f32[64,256]{1,0:T(8,128)S(1)}, u32[]{:S(2)}, u32[]{:S(2)}) collective-permute-start(f32[64,256]{1,0:T(8,128)S(1)} %add_add_fusion.rest_0_), channel_id=1, source_target_pairs={{0,8},{4,12},{8,0},{12,4},{16,24},{20,28},{24,16},{28,20},{1,9},{5... | collective-permute-start | bytes 196616 | tf_op jit(solution)/shard_map/ppermute | solution.py:317
  34.3 14.2 %collective-permute-start.21 = (f32[64,512]{1,0:T(8,128)S(1)}, f32[64,512]{1,0:T(8,128)S(1)}, u32[]{:S(2)}, u32[]{:S(2)}) collective-permute-start(f32[64,512]{1,0:T(8,128)S(1)} %collective-permute-done.13.refs_2_), channel_id=1, source_target_pairs={{0,1},{1,0},{2,3},{3,2},{4,5},{5,4},{6,7},{7,6},{8,9},{9,8},{10,11... | collective-permute-start | bytes 393224 | tf_op jit(solution)/shard_map/ppermute | solution.py:320
  34.3 16.1 %collective-permute-start.17 = (f32[64,512]{1,0:T(8,128)S(1)}, f32[64,512]{1,0:T(8,128)S(1)}, u32[]{:S(2)}, u32[]{:S(2)}) collective-permute-start(f32[64,512]{1,0:T(8,128)S(1)} %collective-permute-done.13.refs_2_), channel_id=1, source_target_pairs={{0,4},{4,0},{8,12},{12,8},{16,20},{20,16},{24,28},{28,24},{1,5},{5... | collective-permute-start | bytes 393224 | tf_op jit(solution)/shard_map/ppermute | solution.py:317
  36.3 14.2 %collective-permute-start.20 = (f32[64,512]{1,0:T(8,128)S(1)}, f32[64,512]{1,0:T(8,128)S(1)}, u32[]{:S(2)}, u32[]{:S(2)}) collective-permute-start(f32[64,512]{1,0:T(8,128)S(1)} %collective-permute-done.12.refs_1_), channel_id=1, source_target_pairs={{0,1},{1,0},{2,3},{3,2},{4,5},{5,4},{6,7},{7,6},{8,9},{9,8},{10,11... | collective-permute-start | bytes 393224 | tf_op jit(solution)/shard_map/ppermute | solution.py:320
  38.9 8.2 %collective-permute-start.14 = (f32[64,512]{1,0:T(8,128)S(1)}, f32[64,512]{1,0:T(8,128)S(1)}, u32[]{:S(2)}, u32[]{:S(2)}) collective-permute-start(f32[64,512]{1,0:T(8,128)S(1)} %collective-permute-done.12.refs_1_), channel_id=1, source_target_pairs={{0,16},{4,20},{8,24},{12,28},{16,0},{20,4},{24,8},{28,12},{1,17},{... | collective-permute-start | bytes 393224 | tf_op jit(solution)/shard_map/ppermute | solution.py:317
  41.5 12.9 %collective-permute-start.16 = (f32[64,512]{1,0:T(8,128)S(1)}, f32[64,512]{1,0:T(8,128)S(1)}, u32[]{:S(2)}, u32[]{:S(2)}) collective-permute-start(f32[64,512]{1,0:T(8,128)S(1)} %collective-permute-done.12.refs_1_), channel_id=1, source_target_pairs={{0,4},{4,0},{8,12},{12,8},{16,20},{20,16},{24,28},{28,24},{1,5},{5... | collective-permute-start | bytes 393224 | tf_op jit(solution)/shard_map/ppermute | solution.py:317
  47.1 7.4 %collective-permute-start.18 = (f32[64,512]{1,0:T(8,128)S(1)}, f32[64,512]{1,0:T(8,128)S(1)}, u32[]{:S(2)}, u32[]{:S(2)}) collective-permute-start(f32[64,512]{1,0:T(8,128)S(1)} %collective-permute-done.14.refs_3_), channel_id=1, source_target_pairs={{0,4},{4,0},{8,12},{12,8},{16,20},{20,16},{24,28},{28,24},{1,5},{5... | collective-permute-start | bytes 393224 | tf_op jit(solution)/shard_map/ppermute | solution.py:317
  54.4 13.2 %collective-permute-start.22 = (f32[64,512]{1,0:T(8,128)S(1)}, f32[64,512]{1,0:T(8,128)S(1)}, u32[]{:S(2)}, u32[]{:S(2)}) collective-permute-start(f32[64,512]{1,0:T(8,128)S(1)} %collective-permute-done.14.refs_3_), channel_id=1, source_target_pairs={{0,1},{1,0},{2,3},{3,2},{4,5},{5,4},{6,7},{7,6},{8,9},{9,8},{10,11... | collective-permute-start | bytes 393224 | tf_op jit(solution)/shard_map/ppermute | solution.py:320
  54.5 12.4 %collective-permute-start.25 = (f32[64,512]{1,0:T(8,128)S(1)}, f32[64,512]{1,0:T(8,128)S(1)}, u32[]{:S(2)}, u32[]{:S(2)}) collective-permute-start(f32[64,512]{1,0:T(8,128)S(1)} %collective-permute-done.17.refs_6_), channel_id=1, source_target_pairs={{0,1},{1,0},{2,3},{3,2},{4,5},{5,4},{6,7},{7,6},{8,9},{9,8},{10,11... | collective-permute-start | bytes 393224 | tf_op jit(solution)/shard_map/ppermute | solution.py:320
  55.0 12.6 %collective-permute-start.24 = (f32[64,512]{1,0:T(8,128)S(1)}, f32[64,512]{1,0:T(8,128)S(1)}, u32[]{:S(2)}, u32[]{:S(2)}) collective-permute-start(f32[64,512]{1,0:T(8,128)S(1)} %collective-permute-done.16.refs_5_), channel_id=1, source_target_pairs={{0,1},{1,0},{2,3},{3,2},{4,5},{5,4},{6,7},{7,6},{8,9},{9,8},{10,11... | collective-permute-start | bytes 393224 | tf_op jit(solution)/shard_map/ppermute | solution.py:320
  55.3 12.3 %collective-permute-start.26 = (f32[64,512]{1,0:T(8,128)S(1)}, f32[64,512]{1,0:T(8,128)S(1)}, u32[]{:S(2)}, u32[]{:S(2)}) collective-permute-start(f32[64,512]{1,0:T(8,128)S(1)} %collective-permute-done.18.refs_7_), channel_id=1, source_target_pairs={{0,1},{1,0},{2,3},{3,2},{4,5},{5,4},{6,7},{7,6},{8,9},{9,8},{10,11... | collective-permute-start | bytes 393224 | tf_op jit(solution)/shard_map/ppermute | solution.py:320
  55.5 13.6 %collective-permute-start.7 = (f32[64,1024]{1,0:T(8,128)S(1)}, f32[64,1024]{1,0:T(8,128)S(1)}, u32[]{:S(2)}, u32[]{:S(2)}) collective-permute-start(f32[64,1024]{1,0:T(8,128)S(1)} %get-tuple-element.41.own), channel_id=1, source_target_pairs={{0,4},{4,0},{8,12},{12,8},{16,20},{20,16},{24,28},{28,24},{1,5},{5... | collective-permute-start | bytes 786440 | tf_op jit(solution)/shard_map/ppermute | solution.py:317
  66.8 6.4 %collective-permute-start.11 = (f32[64,640]{1,0:T(8,128)S(1)}, f32[64,640]{1,0:T(8,128)S(1)}, u32[]{:S(2)}, u32[]{:S(2)}) collective-permute-start(f32[64,640]{1,0:T(8,128)S(1)} %scaled.1.own.middle_own), channel_id=1, source_target_pairs={{0,4},{4,0},{8,12},{12,8},{16,20},{20,16},{24,28},{28,24},{1,5},{5... | collective-permute-start | bytes 491528 | tf_op jit(solution)/shard_map/ppermute | solution.py:317
  79.8 7.4 %collective-permute-start.28 = (f32[64,640]{1,0:T(8,128)S(1)}, f32[64,640]{1,0:T(8,128)S(1)}, u32[]{:S(2)}, u32[]{:S(2)}) collective-permute-start(f32[64,640]{1,0:T(8,128)S(1)} %get-tuple-element.57), channel_id=1, source_target_pairs={{0,2},{1,3},{2,0},{3,1},{4,6},{5,7},{6,4},{7,5},{8,10},{9,11},{10,... | collective-permute-start | bytes 491528 | tf_op jit(solution)/shard_map/ppermute | solution.py:320
  (31 other events, 195.5 us)

commit v2 on v1

v2 whole, which is shorter than its diff:
```python
import functools

import jax
import jax.numpy as jnp
from jax import lax
from jax.experimental import pallas as pl
from jax.experimental.pallas import tpu as pltpu
from jax.sharding import PartitionSpec as P

F32 = jnp.float32
BF16 = jnp.bfloat16
LANES = 128
BLOCK = 256
NN = ((1,), (0,))
NT = ((1,), (1,))
TN = ((0,), (0,))


def halves(x):
    high = x.astype(BF16)
    return high, (x - high.astype(F32)).astype(BF16)


def bdot(a, b, dims=NN):
    return lax.dot_general(a, b, (dims, ((), ())), preferred_element_type=F32)


def dot2(a, b, dims=NN):
    high, low = halves(b)
    return bdot(a, high, dims) + bdot(a, low, dims)


def dot3(a, b, dims=NN):
    ah, al = halves(a)
    bh, bl = halves(b)
    return bdot(ah, bh, dims) + (bdot(ah, bl, dims) + bdot(al, bh, dims))


def vmem_call(body, outs, scratch=(), flops=10**7, name=None, limit=16):
    def call(*operands, needs=()):
        count = len(operands)

        def kernel(*refs):
            body(*refs[:count], *refs[count + len(needs) :])

        vmem = pl.BlockSpec(memory_space=pltpu.VMEM)
        return pl.pallas_call(
            kernel,
            in_specs=[vmem] * count + [pl.BlockSpec(memory_space=pl.ANY)] * len(needs),
            out_specs=[vmem] * len(outs),
            out_shape=[jax.ShapeDtypeStruct(s, d) for s, d in outs],
            scratch_shapes=list(scratch),
            compiler_params=pltpu.CompilerParams(vmem_limit_bytes=limit * 2**20),
            cost_estimate=pl.CostEstimate(flops=flops, bytes_accessed=10**6, transcendentals=0),
            name=name,
        )(*operands, *needs)

    return call


def held(x, *needs, weight=0):
    anywhere = pl.BlockSpec(memory_space=pl.ANY)
    return pl.pallas_call(
        lambda *refs: None,
        in_specs=[anywhere] * (1 + len(needs)),
        out_specs=anywhere,
        out_shape=jax.ShapeDtypeStruct(x.shape, x.dtype),
        input_output_aliases={0: 0},
        compiler_params=pltpu.CompilerParams(vmem_limit_bytes=2**20),
        cost_estimate=pl.CostEstimate(flops=weight, bytes_accessed=0, transcendentals=0),
        name="held",
    )(x, *needs)


def blocks_of(extent):
    size = min(BLOCK, extent)
    return [(start, start + size) for start in range(0, extent, size)]


def widen_body(row_left, out):
    half = out.shape[2]
    start = pl.multiple_of(lax.rem(lax.axis_index("row"), 2) * half, half)
    out[0] = row_left[:, pl.ds(start, half)].astype(F32)


def couple_body(
    tl_hbm, tr_hbm, rl_hbm, rr_hbm, sk_hbm, ready, own_hbm, msg_hbm, tl, tr, rl, rr, sk, own, msg, sems
):
    parity = lax.rem(lax.axis_index("col"), 2)
    rank, nb = rl.shape
    copies = [
        pltpu.make_async_copy(source, target, sems.at[index])
        for index, (source, target) in enumerate(
            (
                (tr_hbm, tr),
                (rr_hbm, rr),
                (tl_hbm, tl),
                (rl_hbm, rl),
                (sk_hbm, sk),
                (msg, msg_hbm),
                (own, own_hbm),
            )
        )
    ]
    for copy in copies[:5]:
        copy.start()
    for copy in copies[:5]:
        copy.wait()

    def crossed(band):
        coupling = bdot(tr[band], rr[...], NT)
        high, low = halves(coupling)
        both = bdot(jnp.concatenate([high, low], 1), tl[band], TN)
        return both[:rank] + both[rank:]

    msg[:, :nb] = crossed(1 - parity)
    probe = bdot(rl[...], sk[...], NT)
    msg[:, nb:] = jnp.concatenate([probe, jnp.zeros_like(probe)], 1)
    copies[5].start()
    own[...] = crossed(parity)
    copies[6].start()
    for copy in copies[5:]:
        copy.wait()


def sketch_body(pieces, x_own, sent, got, x_pair, *rest):
    outs, part = rest[:-1], rest[-1]
    col = lax.axis_index("col")
    parity = lax.rem(col, 2)
    place = col // 2
    rank, nb = x_own.shape
    own, other = x_own[...], got[:, :nb]
    probes = jnp.concatenate([sent[:, nb : nb + rank], got[:, nb : nb + rank]], 0)
    part[...] = dot3(probes, jnp.concatenate([own, other], 0), TN)
    x_pair[pl.ds(pl.multiple_of(parity * rank, rank), rank), :] = own
    x_pair[pl.ds(pl.multiple_of((1 - parity) * rank, rank), rank), :] = other
    slab = nb // pieces
    for step in range(pieces):
        start = pl.multiple_of(jnp.bitwise_xor(place, step) * slab, slab) if pieces > 1 else 0
        outs[step][...] = part[:, pl.ds(start, slab)]


def sum_body(*refs):
    total = refs[0][...]
    for part in refs[1:-1]:
        total = total + part[...]
    refs[-1][...] = total


def project_body(pieces, x_pair, *rest):
    slabs, (sk, crossed, gram) = rest[:pieces], rest[pieces:]
    place = lax.axis_index("col") // 2
    slab = slabs[0].shape[1]
    for step in range(pieces):
        start = pl.multiple_of(jnp.bitwise_xor(place, step) * slab, slab) if pieces > 1 else 0
        sk[:, pl.ds(start, slab)] = slabs[step][...]
    whole = sk[...]
    crossed[...] = dot3(whole, x_pair[...], NT)
    gram[...] = lax.dot_general(
        whole, whole, (NT, ((), ())), precision=lax.Precision.HIGHEST, preferred_element_type=F32
    )


def join_body(first, second, out):
    count = first.shape[0]
    out[:count] = first[...]
    out[count:] = second[...]


def narrow_body(order, *refs):
    blocks, out = refs[:-1], refs[-1]
    half = blocks[0].shape[-1]
    parity = lax.rem(lax.axis_index("col"), 2)
    near_start = pl.multiple_of(lax.rem(lax.axis_index("row"), 2) * half, half)
    far_start = pl.multiple_of(half - near_start, half)
    count = len(blocks) // 4
    for quarter, (side, start) in enumerate(
        ((parity, near_start), (1 - parity, near_start), (parity, far_start), (1 - parity, far_start))
    ):
        index = 0
        for chunk in blocks[quarter * count : (quarter + 1) * count]:
            for row in range(chunk.shape[0]):
                out[order[index], side, :, pl.ds(start, half)] = chunk[row].astype(BF16)
                index += 1


def wide_pulled_body(wide, pulled, high_out, low_out):
    pulled_high, pulled_low = halves(pulled[...])
    for first, last in blocks_of(wide.shape[0]):
        rows = wide[first:last, :]
        product = bdot(rows, pulled_high) + bdot(rows, pulled_low)
        high, low = halves(product)
        high_out[first:last, :] = high
        low_out[first:last, :] = low


def factor_body(bands, gram, sketched, *refs):
    right_rows, (inverse_out, upper_out, slope_out) = refs[:bands], refs[bands:]
    parity = lax.rem(lax.axis_index("col"), 2)
    chosen = right_rows[0][...]
    for band in range(1, bands):
        chosen = jnp.where(parity == band, right_rows[band][...], chosen)
    slope_out[...] = dot3(chosen, sketched[...], NT)
    rank = gram.shape[0]
    lanes = 2 * rank
    group = 4
    tile = 8
    rows = lax.broadcasted_iota(jnp.int32, (rank, lanes), 0)
    cols = lax.broadcasted_iota(jnp.int32, (rank, lanes), 1)
    eye = jnp.where(cols == rows + rank, 1.0, 0.0).astype(F32)
    work = jnp.concatenate([gram[...], jnp.zeros((rank, rank), F32)], 1) + eye
    done = []
    scales = []
    for start in range(0, rank, group):
        top = (start // tile) * tile
        if start == top and start:
            done.append(work[:tile])
            work = work[tile:]
        ids = rows[top:]
        height = rank - top
        columns = [
            jnp.broadcast_to(work[:, start + j : start + j + 1], (height, lanes)) for j in range(group)
        ]
        for j in range(group):
            k = start + j
            at = k - top
            pivot = columns[j][at : at + 1, :]
            inverse = 1.0 / pivot
            scales.append(lax.rsqrt(pivot))
            factor = jnp.where(ids > k, columns[j] * inverse, 0.0)
            for later in range(j + 1, group):
                columns[later] = columns[later] - factor * columns[later][at : at + 1, :]
            work = work - factor * work[at : at + 1, :]
    done.append(work)
    whole = jnp.concatenate(done, 0) * jnp.concatenate(scales, 0)
    upper_out[...] = jnp.where(cols >= rows, whole, 0.0)[:, :rank]
    low = whole[:, rank:]
    inverse_out[...] = dot3(low, low, TN)


def scaled_body(groups, inverse, upper, slope, *rest):
    blocks, out = rest[:groups], rest[groups]
    two = jnp.concatenate(halves(inverse[...]), 0)
    rank, width = blocks[0].shape
    for step in range(groups):
        high, low = halves(blocks[step][...])
        both = bdot(two, high)
        out[:, step * width : (step + 1) * width] = both[:rank] + (both[rank:] + bdot(two[:rank], low))
    out[:, groups * width :] = jnp.concatenate([upper[...], slope[...]], 1)


def band_body(band, inverse, rhs, left, right, base, feed, offset, gain, right_rows):
    rank, nb = right.shape[1:]
    for first, last in blocks_of(nb):
        rows = inverse[band, first:last, :last]
        base[first:last, :] = bdot(rows, rhs[band, :last, :])
        both = bdot(rows, left[band, :, :last], NT)
        for side in range(2):
            high, low = halves(both[:, side * rank : (side + 1) * rank])
            feed[side, first:last, :] = jnp.concatenate([high, high, low], 1)
        right_rows[:, first:last] = bdot(right[band, :, first:], inverse[band, first:, first:last])
    two = jnp.concatenate(halves(right_rows[...]), 0)
    both = bdot(two, rhs[band])
    offset[...] = both[:rank] + both[rank:]
    both = bdot(two, left[band], NT)
    gain[...] = both[:rank] + both[rank:]


def spread_body(inverse, own, spread):
    parity = lax.rem(lax.axis_index("col"), 2)
    rank, nb = own.shape
    two = jnp.concatenate(halves(own[...]), 0)
    for first, last in blocks_of(nb):
        both = bdot(inverse[parity, first:last, :last], two[:, :last], NT)
        spread[:, first:last] = (both[:, :rank] + both[:, rank:]).T


def affine_body(bands, *refs):
    offset, gain = refs[:bands], refs[bands : 2 * bands]
    panel_right, pulled, carry, coeffs, plain, constant, matrix_out = refs[2 * bands :]
    rank = carry.shape[0]
    stacked = jnp.concatenate([panel_right[band] for band in range(bands)], 0)
    both = dot2(stacked, pulled[...])
    for band in range(bands):
        coeffs[band] = both[band * rank : (band + 1) * rank]
    constant_now = None
    matrix = None
    for band in range(bands):
        now = offset[band][...] - dot3(gain[band][:, :rank], coeffs[band])
        plain[band] = now
        feed = gain[band][:, rank:]
        constant_now = now - dot3(feed, constant_now) if band else now
        matrix = -dot3(feed, matrix) if band else -feed
    first = lax.axis_index("row") == 0
    constant[...] = constant_now + jnp.where(first, dot3(matrix, carry[...]), 0.0)
    matrix_out[...] = jnp.where(first, 0.0, matrix)


def stack3(x):
    high, low = halves(x)
    return jnp.concatenate([high, low, high], 0)


def weight_body(bands, *refs):
    gain = refs[:bands]
    own, other, wp_high, wp_low, constant, matrix, weights, pack = refs[bands:]
    parity = lax.rem(lax.axis_index("col"), 2)
    rank = own.shape[0]
    count, width = wp_high.shape
    sides = [middle[:, :count] for middle in (own, other)]
    highs, lows = zip(*[halves(side) for side in sides])
    upper = bdot(jnp.concatenate(highs + lows, 0), wp_high[...])
    lower = bdot(jnp.concatenate(highs, 0), wp_low[...])
    own_first = upper[: bands * rank] + (upper[bands * rank :] + lower)
    own_weight, other_weight = own_first[:rank], own_first[rank:]
    ordered = []
    slopes = []
    for band in range(bands):
        ordered.append(jnp.where(parity == band, own_weight, other_weight))
        weights[band] = ordered[band]
        if band:
            slopes = [-dot3(gain[band][:, rank:], slope) for slope in slopes]
        ends = [middle[:, count + rank : count + 2 * rank] for middle in (own, other)]
        slopes.append(jnp.where(parity == band, ends[0], ends[1]))
    pack[:, :width] = constant[...] + dot3(jnp.concatenate(slopes, 1), jnp.concatenate(ordered, 0))
    pack[:, width:] = jnp.concatenate([matrix[...], jnp.zeros((rank, LANES - rank), F32)], 1)


def compose_body(bit, first, width, near, group, other, near_out, group_out):
    rank = group.shape[0]
    upper = lax.rem(lax.axis_index("row") // bit, 2) == 1

    def chained(then, before):
        moved = dot3(then[:, width : width + rank], before)
        lanes = lax.broadcasted_iota(jnp.int32, moved.shape, 1)
        return moved + jnp.where(lanes < width, then, 0.0)

    own, far = group[...], other[...]
    group_out[...] = chained(jnp.where(upper, own, far), jnp.where(upper, far, own))
    if first:
        lanes = lax.broadcasted_iota(jnp.int32, own.shape, 1)
        rows = lax.broadcasted_iota(jnp.int32, own.shape, 0)
        identity = jnp.where(lanes == rows + width, 1.0, 0.0).astype(F32)
        near_out[...] = jnp.where(upper, far, identity)
    else:
        near_out[...] = jnp.where(upper, chained(near[...], far), near[...])


def partial_body(bands, *refs):
    base, feed = refs[:bands], refs[bands : 2 * bands]
    own, other, weights, coeffs, plain, middle_own, middle_other, slab, out, offsets, schur = refs[2 * bands :]
    parity = lax.rem(lax.axis_index("col"), 2)
    nb = out.shape[1]
    rank = schur.shape[1]
    count, extent = slab.shape
    for band in range(bands):
        weight = weights[band]
        weight_three = stack3(weight)
        coeffs_three = stack3(coeffs[band])
        high, low = halves(jnp.where(parity == band, own[...], other[...]))
        spread = jnp.concatenate([high, high, low], 0)
        for first, last in blocks_of(nb):
            out[band, first:last, :] = (
                base[band][first:last, :]
                + bdot(spread[:, first:last], weight_three, TN)
                - bdot(feed[band][0, first:last, :], coeffs_three)
            )
        slope = jnp.where(
            parity == band,
            middle_own[:, count + rank : count + 2 * rank],
            middle_other[:, count + rank : count + 2 * rank],
        )
        offsets[band] = plain[band] + dot3(slope, weight)
    width = schur.shape[2]
    if extent == width:
        columns = slab[...]
    else:
        start = pl.multiple_of(lax.axis_index("col") * width, width)
        columns = slab[:, pl.ds(start, width)]
    for side, middle in ((parity, middle_own), (1 - parity, middle_other)):
        basis_side = dot3(middle[:, count : count + rank], middle[:, :count])
        both = bdot(jnp.concatenate(halves(basis_side), 0), columns)
        schur[side] = both[:rank] + both[rank:]


def finish_body(bands, bit, *refs):
    feed, gain = refs[:bands], refs[bands : 2 * bands]
    partial, offsets, near, other, carry, solved_hbm, states, solved, sems = refs[2 * bands :]
    _, nb, width = partial.shape
    rank = carry.shape[0]
    upper = lax.rem(lax.axis_index("row") // bit, 2) == 1
    prior = jnp.where(upper, other[...], carry[...])
    prior = dot3(near[:, width : width + rank], prior) + near[:, :width]
    threes = []
    for band in range(bands):
        threes.append(stack3(prior))
        prior = offsets[band] - dot3(gain[band][:, rank:], prior)
        states[band] = prior
    copies = []
    for band in range(bands):
        for first, last in blocks_of(nb):
            solved[band, first:last, :] = (
                partial[band, first:last, :] - bdot(feed[band][1, first:last, :], threes[band])
            ).astype(BF16)
            copy = pltpu.make_async_copy(
                solved.at[band, first:last, :],
                solved_hbm.at[band, first:last, :],
                sems.at[len(copies)],
            )
            copy.start()
            copies.append(copy)
    for copy in copies:
        copy.wait()


def shards(
    tile_left,
    tile_right,
    row_left,
    row_right,
    sketch,
    panel_left,
    panel_right,
    pivot_inverse,
    band_inverse,
    link_left,
    link_right,
    pivot_rhs,
    band_rhs,
    carry_in,
):
    cols = lax.axis_size("col")
    rows = lax.axis_size("row")
    groups = cols // 2
    col = lax.axis_index("col")
    bands, nb, rank = tile_left.shape[1:]
    width = pivot_rhs.shape[1]
    slab = nb // groups
    count = cols * rank

    def swap(x, step):
        return lax.ppermute(x, "col", [(c, c ^ step) for c in range(cols)])

    def row_swap(x, step):
        return lax.ppermute(x, "row", [(r, r ^ step) for r in range(rows)])

    def turned(x):
        return jnp.swapaxes(x, -1, -2)

    def joined(first, second, *needs):
        shape = (2 * first.shape[0],) + first.shape[1:]
        return vmem_call(join_body, [(shape, F32)], name="join")(first, second, needs=needs)[0]

    row_left_t = turned(row_left[0])
    (wide,) = vmem_call(widen_body, [((1, rank, nb // 2), F32)], name="widen")(row_left_t)
    order = [0]
    reach = groups // 2
    def hbm(count):
        return [pl.BlockSpec(memory_space=pltpu.HBM)] * count

    x_own, x_sent = pl.pallas_call(
        couple_body,
        in_specs=hbm(5) + [pl.BlockSpec(memory_space=pl.ANY)],
        out_specs=hbm(2),
        out_shape=[
            jax.ShapeDtypeStruct((rank, nb), F32),
            jax.ShapeDtypeStruct((rank, nb + LANES), F32),
        ],
        scratch_shapes=[pltpu.VMEM((bands, rank, nb), BF16)] * 2
        + [pltpu.VMEM((rank, nb), BF16)] * 3
        + [
            pltpu.VMEM((rank, nb), F32),
            pltpu.VMEM((rank, nb + LANES), F32),
            pltpu.SemaphoreType.DMA((7,)),
        ],
        compiler_params=pltpu.CompilerParams(vmem_limit_bytes=60 * 2**20),
        name="couple",
    )(
        turned(tile_left[0]),
        turned(tile_right[0]),
        row_left_t,
        turned(row_right[0]),
        turned(sketch),
        wide,
    )
    x_got = swap(x_sent, 1)

    pivot_solution = jnp.dot(pivot_inverse, pivot_rhs, preferred_element_type=F32).astype(BF16)
    pulled = bdot(pivot_inverse, pivot_solution, TN)

    def one_band(band, *needs):
        shapes = [(nb, width), (2, nb, 3 * rank), (rank, width), (rank, 2 * rank), (rank, nb)]
        return vmem_call(
            functools.partial(band_body, band),
            [(shape, BF16 if index == 1 else F32) for index, shape in enumerate(shapes)],
            flops=2 * 10**9,
            name="band",
        )(band_inverse, band_rhs, left_t, right_t, needs=needs)

    if reach:
        wide = joined(wide, swap(wide, 2 * reach))
        order = order + [place ^ reach for place in order]
        reach //= 2
    pieces = groups if slab % LANES == 0 else 1
    parts = vmem_call(
        functools.partial(sketch_body, pieces),
        [((2 * rank, nb), F32)] + [((rank, nb // pieces), F32)] * pieces,
        [pltpu.VMEM((rank, nb), F32)],
        name="sketch",
    )(x_own, x_sent, x_got, needs=(pulled, wide))
    x_pair, parts = parts[0], parts[1:]

    left_t = jnp.concatenate([turned(panel_left), turned(link_left)], 1)
    right_t = turned(link_right)
    whole_bands = []
    for band in range(bands):
        whole_bands.append(one_band(band, x_pair, *(last[-1] for last in whole_bands[-1:])))
    bases, feeds, offsets_in, gains, right_rows = zip(*whole_bands)
    coeffs, plain, constant, matrix = vmem_call(
        functools.partial(affine_body, bands),
        [((bands, rank, width), F32)] * 2 + [((rank, width), F32), ((rank, rank), F32)],
        name="affine",
    )(*offsets_in, *gains, turned(panel_right), pulled, carry_in)

    if pieces > 1:
        (total,) = vmem_call(sum_body, [((rank, slab), F32)], name="sum")(
            parts[0],
            *[swap(parts[step], 2 * step) for step in range(1, pieces)],
            needs=(wide, matrix),
        )
        slabs = [total] + [swap(total, 2 * step) for step in range(1, pieces)]
    else:
        members = [list(range(side, cols, 2)) for side in range(2)]
        total = lax.psum(parts[0], "col", axis_index_groups=members)
        slabs = [total]
    while reach:
        wide = joined(wide, swap(wide, 2 * reach), total)
        order = order + [place ^ reach for place in order]
        reach //= 2
    wide_other = held(swap(wide, 1), weight=0)
    sketched, crossed, gram = vmem_call(
        functools.partial(project_body, pieces),
        [((rank, nb), F32), ((rank, 2 * rank), F32), ((rank, rank), F32)],
        name="project",
    )(x_pair, *slabs)
    crossed_all = [crossed] + [swap(crossed, 2 * step) for step in range(1, groups)]
    inverse_gram, upper, slope = vmem_call(
        functools.partial(factor_body, bands), [((rank, rank), F32)] * 3, flops=3 * 10**10, name="factor"
    )(gram, sketched, *right_rows)
    (middle,) = vmem_call(
        functools.partial(scaled_body, groups), [((rank, count + LANES), F32)], name="scaled"
    )(inverse_gram, upper, slope, *crossed_all)
    middle_other = held(swap(middle, 1), weight=3 * 10**10)
    (spread,) = vmem_call(spread_body, [((rank, nb), F32)], name="spread")(
        band_inverse, sketched, needs=(middle, wide_other)
    )
    spread_other = swap(spread, 1)

    (wide,) = vmem_call(
        functools.partial(narrow_body, order), [((groups, 2, rank, nb), BF16)], name="narrow"
    )(wide, wide_other, row_swap(wide, 1), row_swap(wide_other, 1))
    wide = wide.reshape(count, nb)
    wp_high, wp_low = vmem_call(
        wide_pulled_body, [((count, width), BF16)] * 2, name="wide_pulled"
    )(wide, pulled)
    weights, pack = vmem_call(
        functools.partial(weight_body, bands),
        [((bands, rank, width), F32), ((rank, width + LANES), F32)],
        name="weight",
    )(*gains, middle, middle_other, wp_high, wp_low, constant, matrix)

    near, group = pack, pack
    step = 1
    while 2 * step < rows:
        near, group = vmem_call(
            functools.partial(compose_body, step, step == 1, width),
            [((rank, width + LANES), F32)] * 2,
            name="compose",
        )(near, group, row_swap(group, step))
        step *= 2
    arrived = row_swap(group[:, :width], step)

    own_slab = wide
    if (nb // cols) % LANES:
        own_slab = lax.dynamic_slice_in_dim(wide, col * (nb // cols), nb // cols, 1)
    partial, offsets, schur = vmem_call(
        functools.partial(partial_body, bands),
        [
            ((bands, nb, width), F32),
            ((bands, rank, width), F32),
            ((bands, rank, nb // cols), F32),
        ],
        flops=10**9,
        name="partial",
    )(
        *bases,
        *feeds,
        spread,
        spread_other,
        weights,
        coeffs,
        plain,
        middle,
        middle_other,
        own_slab,
        needs=(group,),
    )
    vmem = pl.BlockSpec(memory_space=pltpu.VMEM)
    solved, states = pl.pallas_call(
        functools.partial(finish_body, bands, step),
        in_specs=[vmem] * (2 * bands + 5),
        out_specs=[pl.BlockSpec(memory_space=pltpu.HBM), vmem],
        out_shape=[
            jax.ShapeDtypeStruct((bands, nb, width), BF16),
            jax.ShapeDtypeStruct((bands, rank, width), F32),
        ],
        scratch_shapes=[
            pltpu.VMEM((bands, nb, width), BF16),
            pltpu.SemaphoreType.DMA((bands * len(blocks_of(nb)),)),
        ],
        compiler_params=pltpu.CompilerParams(vmem_limit_bytes=16 * 2**20),
        cost_estimate=pl.CostEstimate(flops=10**9, bytes_accessed=10**6, transcendentals=0),
        name="finish",
    )(*feeds, *gains, partial, offsets, near, arrived, carry_in)
    return (pivot_solution, turned(schur), solved, states)


def solution(mesh):
    return jax.shard_map(
        shards,
        mesh=mesh,
        in_specs=(
            P("col", "row", None, None),
            P("col", "row", None, None),
            P("col", None, None),
            P("col", None, None),
            P(),
            P("row", None, None),
            P("row", None, None),
            P(),
            P("row", None, None),
            P("row", None, None),
            P("row", None, None),
            P(None, "col"),
            P("row", None, "col"),
            P(None, "col"),
        ),
        out_specs=(
            P(None, "col"),
            P("row", "col", None),
            P("row", None, "col"),
            P("row", None, "col"),
        ),
        check_vma=False,
    )
```

time: 90.1 us -> 60.7 us (0.67)
  waiting for transfers between devices: 21.5 us -> 7.16 us
  local copies, waits for them, and re-layouts: 14.6 us -> 1.16 us
  starting transfers between devices: 30.4 us -> 27.8 us
  matrix products: 2.54 us -> 3.76 us
    ppermute x19 -> x15, waiting for transfers between devices: 19.8 us -> 4.82 us  [swap(): return lax.ppermute(x, 'col', [(c, c ^ step) for c in range(cols)])]
    unnamed x52 -> x28, local copies, waits for them, and re-layouts: 14.5 us -> 1.15 us
    ppermute x19 -> x15, starting transfers between devices: 27.7 us -> 25.7 us  [swap(): return lax.ppermute(x, 'col', [(c, c ^ step) for c in range(cols)])]
    dot_general x1, matrix products: 1.25 us -> 2.47 us  [shards(): jnp.dot(pivot_inverse, pivot_rhs, preferred_element_type=F32).astype(BF16)]
    ppermute x10 -> x4, waiting for transfers between devices: 1.77 us -> 2.34 us  [row_swap(): return lax.ppermute(x, 'row', [(r, r ^ step) for r in range(rows)])]
    ppermute x10 -> x4, starting transfers between devices: 2.69 us -> 2.13 us  [row_swap(): return lax.ppermute(x, 'row', [(r, r ^ step) for r in range(rows)])]
    pallas_call x14 -> x21, Pallas kernels: 19.8 us -> 19.6 us  [the longest x17 14 us: call(): pl.pallas_call(kernel, in_specs=[vmem] * count + [pl.BlockSpec(memory_spa...]
  transfers between devices with their start and end apart: 29 -> 19, of which waited for: 8 -> 7; matrix products, arithmetic and copies ran while one was open for 3% -> 6% of each run, Pallas kernels for 14% -> 28%
where the time goes in v2:
time: 60.7 us; the launch traced here: 60.4 us
  starting transfers between devices  27.8 us (46%)
  Pallas kernels  19.6 us (32%)
  waiting for transfers between devices  7.16 us (12%)
  matrix products  3.76 us (6%)
  local copies, waits for them, and re-layouts  1.16 us (2%)
  between operations  0.97 us (2%)
    ppermute x15, starting transfers between devices, swap(): return lax.ppermute(x, 'col', [(c, c ^ step) for c in range(cols)])  25.7 us
    pallas_call x17, Pallas kernels, call(): pl.pallas_call(kernel, in_specs=[vmem] * count + [pl.BlockSpec(memory_spa...  14 us
    ppermute x15, waiting for transfers between devices, swap(): return lax.ppermute(x, 'col', [(c, c ^ step) for c in range(cols)])  4.82 us
    pallas_call x1, Pallas kernels, shards(): pl.pallas_call(couple_body, in_specs=hbm(5) + [pl.BlockSpec(memory_space=...  2.8 us
    pallas_call x1, Pallas kernels, shards(): pl.pallas_call(functools.partial(finish_body, bands, step), in_specs=[vme...  2.73 us
    dot_general x1, matrix products, shards(): jnp.dot(pivot_inverse, pivot_rhs, preferred_element_type=F32).astype(BF16)  2.47 us
    ppermute x4, waiting for transfers between devices, row_swap(): return lax.ppermute(x, 'row', [(r, r ^ step) for r in range(rows)])  2.34 us
    ppermute x4, starting transfers between devices, row_swap(): return lax.ppermute(x, 'row', [(r, r ^ step) for r in range(rows)])  2.13 us
  transfers between devices with their start and end apart: 19, of which 7 were waited for; matrix products, arithmetic and copies ran while one was open for 6% of the time, Pallas kernels for 28%

profile of v2, /device:TPU:0, one launch (start us, length us, event | category | flops | bytes accessed | tf_op | source)
XLA Modules:
  0.0 60.4 jit_solution(16265290481741267714)
XLA Ops:
  1.7 4.1 %collective-permute-start.1 = (f32[1,64,512]{2,1,0:T(8,128)S(1)}, f32[1,64,512]{2,1,0:T(8,128)S(1)}, u32[]{:S(2)}, u32[]{:S(2)}) collective-permute-start(f32[1,64,512]{2,1,0:T(8,128)S(1)} %widen.1.ready.refs_0_), channel_id=1, source_target_pairs={{0,16},{4,20},{8,24},{12,28},{16,0},{20,4},{24,8},{28,12},{1,17},{... | collective-permute-start | bytes 393224 | tf_op jit(solution)/shard_map/ppermute | solution.py:442
  5.8 2.8 %couple.1 = (f32[64,1024]{1,0:T(8,128)}, f32[64,1152]{1,0:T(8,128)}) custom-call(bf16[2,64,1024]{2,1,0:T(8,128)(2,1)} %bitcast.32, bf16[2,64,1024]{2,1,0:T(8,128)(2,1)} %bitcast.33, bf16[64,1024]{1,0:T(8,128)(2,1)} %bitcast.29, bf16[64,1024]{1,0:T(8,128)(2,1)} %bitcast.36, bf16[64,1024]{1,0:T(8,128)(2,1)} %bitcast.37, f32[1,64,512]{2,1,0:T(8,128)} %copy-done.3), custom_call_target="tpu_custom_call" | custom-call | tf_op jit(solution)/shard_map/couple/pallas_call | solution.py:461
  8.6 1.6 %collective-permute-start = (f32[64,1152]{1,0:T(8,128)}, f32[64,1152]{1,0:T(8,128)S(1)}, u32[]{:S(2)}, u32[]{:S(2)}) collective-permute-start(f32[64,1152]{1,0:T(8,128)} %get-tuple-element.43.refs_1_), channel_id=1, source_target_pairs={{0,4},{4,0},{8,12},{12,8},{16,20},{20,16},{24,28},{28,24},{1,5},{5... | collective-permute-start | bytes 884744 | tf_op jit(solution)/shard_map/ppermute | solution.py:442
  10.2 2.5 %convolution_convert_fusion = bf16[1024,512]{1,0:T(8,128)(2,1)S(1)} fusion(bf16[1024,1024]{1,0:T(8,128)(2,1)S(1)} %copy-done, bf16[1024,512]{1,0:T(8,128)(2,1)} %param.25), kind=kOutput, calls=%fused_computation.1 | convolution fusion | flops 1074266112 | bytes 4194304 | tf_op jit(solution)/shard_map/dot_general | solution.py:488
  12.8 1.3 %convolution_bitcast_fusion.refs_3_.refs_5_.refs_1_ = f32[1024,512]{1,0:T(8,128)S(1)} fusion(bf16[1024,512]{1,0:T(8,128)(2,1)S(1)} %convolution_convert_fusion, bf16[1024,1024]{1,0:T(8,128)(2,1)S(1)} %copy-done), kind=kOutput, calls=%fused_computation | convolution fusion | flops 1073741824 | bytes 5242880 | tf_op jit(solution)/shard_map/dot_general | solution.py:25
  14.2 1.6 %collective-permute-start.11 = (f32[2,64,512]{2,1,0:T(8,128)S(1)}, f32[2,64,512]{2,1,0:T(8,128)S(1)}, u32[]{:S(2)}, u32[]{:S(2)}) collective-permute-start(f32[2,64,512]{2,1,0:T(8,128)S(1)} %join.2.refs_4_.refs_0_), channel_id=1, source_target_pairs={{0,8},{4,12},{8,0},{12,4},{16,24},{20,28},{24,16},{28,20},{1,9},{5... | collective-permute-start | bytes 786440 | tf_op jit(solution)/shard_map/ppermute | solution.py:442
  15.9 1.5 %collective-permute-done.refs_2_ = f32[64,1152]{1,0:T(8,128)S(1)} collective-permute-done((f32[64,1152]{1,0:T(8,128)}, f32[64,1152]{1,0:T(8,128)S(1)}, u32[]{:S(2)}, u32[]{:S(2)}) %collective-permute-start) | collective-permute-done | bytes 294944 | tf_op jit(solution)/shard_map/ppermute | solution.py:442
  17.8 1.6 %collective-permute-start.2 = (f32[64,256]{1,0:T(8,128)S(1)}, f32[64,256]{1,0:T(8,128)S(1)}, u32[]{:S(2)}, u32[]{:S(2)}) collective-permute-start(f32[64,256]{1,0:T(8,128)S(1)} %get-tuple-element.51), channel_id=1, source_target_pairs={{0,8},{4,12},{8,0},{12,4},{16,24},{20,28},{24,16},{28,20},{1,9},{5... | collective-permute-start | bytes 196616 | tf_op jit(solution)/shard_map/ppermute | solution.py:442
  20.3 2.0 %collective-permute-start.4 = (f32[64,256]{1,0:T(8,128)S(1)}, f32[64,256]{1,0:T(8,128)S(1)}, u32[]{:S(2)}, u32[]{:S(2)}) collective-permute-start(f32[64,256]{1,0:T(8,128)S(1)} %get-tuple-element.53), channel_id=1, source_target_pairs={{0,24},{4,28},{8,16},{12,20},{16,8},{20,12},{24,0},{28,4},{1,25},{... | collective-permute-start | bytes 196616 | tf_op jit(solution)/shard_map/ppermute | solution.py:442
  22.2 1.6 %band.2 = (f32[1024,512]{1,0:T(8,128)S(1)}, bf16[2,1024,192]{2,1,0:T(8,128)(2,1)S(1)}, f32[64,512]{1,0:T(8,128)S(1)}, f32[64,128]{1,0:T(8,128)S(1)}, f32[64,1024]{1,0:T(8,128)S(1)}) custom-call(bf16[2,1024,1024]{2,1,0:T(8,128)(2,1)S(1)} %copy-done.1, bf16[2,1024,512]{2,1,0:T(8,128)(2,1)S(1)} %copy-done.2, bf16[2,128,1024]{2,1,0:T(8,128)(2,1)S(1)} %pad_maximum_fusion.refs_2_, ...), custom_call_target="tpu_custom_call" | custom-call | flops 2000000000 | bytes 1000000 | tf_op jit(solution)/shard_map/band/pallas_call | solution.py:47
  23.9 1.6 %band.3 = (f32[1024,512]{1,0:T(8,128)S(1)}, bf16[2,1024,192]{2,1,0:T(8,128)(2,1)S(1)}, f32[64,512]{1,0:T(8,128)S(1)}, f32[64,128]{1,0:T(8,128)S(1)}, f32[64,1024]{1,0:T(8,128)S(1)}) custom-call(bf16[2,1024,1024]{2,1,0:T(8,128)(2,1)S(1)} %copy-done.1, bf16[2,1024,512]{2,1,0:T(8,128)(2,1)S(1)} %copy-done.2, bf16[2,128,1024]{2,1,0:T(8,128)(2,1)S(1)} %pad_maximum_fusion.refs_2_, ...), custom_call_target="tpu_custom_call" | custom-call | flops 2000000000 | bytes 1000000 | tf_op jit(solution)/shard_map/band/pallas_call | solution.py:47
  26.7 2.8 %collective-permute-start.7 = (f32[64,256]{1,0:T(8,128)S(1)}, f32[64,256]{1,0:T(8,128)S(1)}, u32[]{:S(2)}, u32[]{:S(2)}) collective-permute-start(f32[64,256]{1,0:T(8,128)S(1)} %sum.1.refs_1_.refs_2_), channel_id=1, source_target_pairs={{0,24},{4,28},{8,16},{12,20},{16,8},{20,12},{24,0},{28,4},{1,25},{... | collective-permute-start | bytes 196616 | tf_op jit(solution)/shard_map/ppermute | solution.py:442
  29.5 1.7 %collective-permute-start.5 = (f32[64,256]{1,0:T(8,128)S(1)}, f32[64,256]{1,0:T(8,128)S(1)}, u32[]{:S(2)}, u32[]{:S(2)}) collective-permute-start(f32[64,256]{1,0:T(8,128)S(1)} %sum.1.refs_1_.refs_2_), channel_id=1, source_target_pairs={{0,8},{4,12},{8,0},{12,4},{16,24},{20,28},{24,16},{28,20},{1,9},{5... | collective-permute-start | bytes 196616 | tf_op jit(solution)/shard_map/ppermute | solution.py:442
  31.2 1.8 %collective-permute-start.12 = (f32[4,64,512]{2,1,0:T(8,128)S(1)}, f32[4,64,512]{2,1,0:T(8,128)S(1)}, u32[]{:S(2)}, u32[]{:S(2)}) collective-permute-start(f32[4,64,512]{2,1,0:T(8,128)S(1)} %join.3.refs_0_), channel_id=1, source_target_pairs={{0,4},{4,0},{8,12},{12,8},{16,20},{20,16},{24,28},{28,24},{1,5},{5... | collective-permute-start | bytes 1572872 | tf_op jit(solution)/shard_map/ppermute | solution.py:442
  33.3 1.4 %collective-permute-done.6.refs_3_ = f32[64,256]{1,0:T(8,128)S(1)} collective-permute-done((f32[64,256]{1,0:T(8,128)S(1)}, f32[64,256]{1,0:T(8,128)S(1)}, u32[]{:S(2)}, u32[]{:S(2)}) %collective-permute-start.6) | collective-permute-done | bytes 65568 | tf_op jit(solution)/shard_map/ppermute | solution.py:442
  35.3 2.4 %collective-permute-start.10 = (f32[64,128]{1,0:T(8,128)S(1)}, f32[64,128]{1,0:T(8,128)S(1)}, u32[]{:S(2)}, u32[]{:S(2)}) collective-permute-start(f32[64,128]{1,0:T(8,128)S(1)} %get-tuple-element.65.refs_3_), channel_id=1, source_target_pairs={{0,24},{4,28},{8,16},{12,20},{16,8},{20,12},{24,0},{28,4},{1,25},{... | collective-permute-start | bytes 98312 | tf_op jit(solution)/shard_map/ppermute | solution.py:442
  37.7 2.1 %collective-permute-start.8 = (f32[64,128]{1,0:T(8,128)S(1)}, f32[64,128]{1,0:T(8,128)S(1)}, u32[]{:S(2)}, u32[]{:S(2)}) collective-permute-start(f32[64,128]{1,0:T(8,128)S(1)} %get-tuple-element.65.refs_3_), channel_id=1, source_target_pairs={{0,8},{4,12},{8,0},{12,4},{16,24},{20,28},{24,16},{28,20},{1,9},{5... | collective-permute-start | bytes 98312 | tf_op jit(solution)/shard_map/ppermute | solution.py:442
  39.8 2.9 %factor.1 = (f32[64,64]{1,0:T(8,128)S(1)}, f32[64,64]{1,0:T(8,128)S(1)}, f32[64,64]{1,0:T(8,128)S(1)}) custom-call(f32[64,64]{1,0:T(8,128)S(1)} %get-tuple-element.60.refs_0_, f32[64,1024]{1,0:T(8,128)S(1)} %get-tuple-element.59.refs_1_, f32[64,1024]{1,0:T(8,128)S(1)} %get-tuple-element.46.refs_5_.refs_2_, f32[64,1024]{1,0:T(8,128)S(1)} %get-tuple-element.61.refs_3_), custom_call_target="tpu_custom_call" | custom-call | flops 30000001024 | bytes 1000000 | tf_op jit(solution)/shard_map/factor/pallas_call | solution.py:47
  42.9 1.9 %collective-permute-start.14 = (f32[64,640]{1,0:T(8,128)S(1)}, f32[64,640]{1,0:T(8,128)S(1)}, u32[]{:S(2)}, u32[]{:S(2)}) collective-permute-start(f32[64,640]{1,0:T(8,128)S(1)} %scaled.1.refs_2_.refs_9_), channel_id=1, source_target_pairs={{0,4},{4,0},{8,12},{12,8},{16,20},{20,16},{24,28},{28,24},{1,5},{5... | collective-permute-start | bytes 491528 | tf_op jit(solution)/shard_map/ppermute | solution.py:442
  46.0 1.3 %collective-permute-start.13 = (f32[64,1024]{1,0:T(8,128)S(1)}, f32[64,1024]{1,0:T(8,128)S(1)}, u32[]{:S(2)}, u32[]{:S(2)}) collective-permute-start(f32[64,1024]{1,0:T(8,128)S(1)} %spread.1.refs_4_), channel_id=1, source_target_pairs={{0,4},{4,0},{8,12},{12,8},{16,20},{20,16},{24,28},{28,24},{1,5},{5... | collective-permute-start | bytes 786440 | tf_op jit(solution)/shard_map/ppermute | solution.py:442
  50.5 1.4 %collective-permute-done.17.refs_2_ = f32[64,640]{1,0:T(8,128)S(1)} collective-permute-done((f32[64,640]{1,0:T(8,128)S(1)}, f32[64,640]{1,0:T(8,128)S(1)}, u32[]{:S(2)}, u32[]{:S(2)}) %collective-permute-start.17) | collective-permute-done | bytes 163872 | tf_op jit(solution)/shard_map/ppermute | solution.py:445
  52.1 1.5 %collective-permute-start.18 = (f32[64,512]{1,0:T(8,128)S(1)}, f32[64,512]{1,0:T(8,128)S(1)}, u32[]{:S(2)}, u32[]{:S(2)}) collective-permute-start(f32[64,512]{1,0:T(8,128)S(1)} %slice.3), channel_id=1, source_target_pairs={{0,2},{1,3},{2,0},{3,1},{4,6},{5,7},{6,4},{7,5},{8,10},{9,11},{10,... | collective-permute-start | bytes 393224 | tf_op jit(solution)/shard_map/ppermute | solution.py:445
  54.3 2.5 %partial.1 = (f32[2,1024,512]{2,1,0:T(8,128)S(1)}, f32[2,64,512]{2,1,0:T(8,128)S(1)}, f32[2,64,128]{2,1,0:T(8,128)}) custom-call(f32[1024,512]{1,0:T(8,128)S(1)} %get-tuple-element.45.refs_0_, f32[1024,512]{1,0:T(8,128)S(1)} %get-tuple-element.47.refs_1_, bf16[2,1024,192]{2,1,0:T(8,128)(2,1)S(1)} %get-tuple-element.48.refs_2_.refs_0_, ...), custom_call_target="tpu_custom_call" | custom-call | flops 1000000000 | bytes 1000000 | tf_op jit(solution)/shard_map/partial/pallas_call | solution.py:47
  57.7 2.7 %finish.1 = (bf16[2,1024,512]{2,1,0:T(8,128)(2,1)}, f32[2,64,512]{2,1,0:T(8,128)}) custom-call(bf16[2,1024,192]{2,1,0:T(8,128)(2,1)S(1)} %get-tuple-element.48.refs_2_.refs_0_, bf16[2,1024,192]{2,1,0:T(8,128)(2,1)S(1)} %get-tuple-element.49.refs_3_.refs_1_, f32[64,128]{1,0:T(8,128)S(1)} %get-tuple-element.56.refs_2_.refs_0_, ...), custom_call_target="tpu_custom_call" | custom-call | flops 1000000000 | bytes 1000000 | tf_op jit(solution)/shard_map/finish/pallas_call | solution.py:609
  (67 shorter events, 10.8 us)
Async XLA Ops:
  0.6 9.6 %copy-start = (bf16[1024,1024]{1,0:T(8,128)(2,1)S(1)}, bf16[1024,1024]{1,0:T(8,128)(2,1)}, u32[]{:S(2)}) copy-start(bf16[1024,1024]{1,0:T(8,128)(2,1)} %param.21) | copy-start | bytes 6291460
  1.7 12.4 %collective-permute-start.1 = (f32[1,64,512]{2,1,0:T(8,128)S(1)}, f32[1,64,512]{2,1,0:T(8,128)S(1)}, u32[]{:S(2)}, u32[]{:S(2)}) collective-permute-start(f32[1,64,512]{2,1,0:T(8,128)S(1)} %widen.1.ready.refs_0_), channel_id=1, source_target_pairs={{0,16},{4,20},{8,24},{12,28},{16,0},{20,4},{24,8},{28,12},{1,17},{... | collective-permute-start | bytes 393224 | tf_op jit(solution)/shard_map/ppermute | solution.py:442
  8.6 8.7 %collective-permute-start = (f32[64,1152]{1,0:T(8,128)}, f32[64,1152]{1,0:T(8,128)S(1)}, u32[]{:S(2)}, u32[]{:S(2)}) collective-permute-start(f32[64,1152]{1,0:T(8,128)} %get-tuple-element.43.refs_1_), channel_id=1, source_target_pairs={{0,4},{4,0},{8,12},{12,8},{16,20},{20,16},{24,28},{28,24},{1,5},{5... | collective-permute-start | bytes 884744 | tf_op jit(solution)/shard_map/ppermute | solution.py:442
  12.7 4.6 %copy-start.8 = (f32[64,1152]{1,0:T(8,128)S(1)}, f32[64,1152]{1,0:T(8,128)}, u32[]{:S(2)}) copy-start(f32[64,1152]{1,0:T(8,128)} %get-tuple-element.43.refs_1_) | copy-start | bytes 884740
  12.8 9.5 %copy-start.2 = (bf16[2,1024,512]{2,1,0:T(8,128)(2,1)S(1)}, bf16[2,1024,512]{2,1,0:T(8,128)(2,1)}, u32[]{:S(2)}) copy-start(bf16[2,1024,512]{2,1,0:T(8,128)(2,1)} %refs_1_.3) | copy-start | bytes 6291460
  14.1 8.1 %copy-start.1 = (bf16[2,1024,1024]{2,1,0:T(8,128)(2,1)S(1)}, bf16[2,1024,1024]{2,1,0:T(8,128)(2,1)}, u32[]{:S(2)}) copy-start(bf16[2,1024,1024]{2,1,0:T(8,128)(2,1)} %refs_0_.5) | copy-start | bytes 12582916
  14.2 8.1 %copy-start.5 = (bf16[2,1024,64]{1,2,0:T(8,128)(2,1)S(1)}, bf16[2,1024,64]{1,2,0:T(8,128)(2,1)}, u32[]{:S(2)}) copy-start(bf16[2,1024,64]{1,2,0:T(8,128)(2,1)} %param.24) | copy-start | bytes 786436
  14.2 17.0 %collective-permute-start.11 = (f32[2,64,512]{2,1,0:T(8,128)S(1)}, f32[2,64,512]{2,1,0:T(8,128)S(1)}, u32[]{:S(2)}, u32[]{:S(2)}) collective-permute-start(f32[2,64,512]{2,1,0:T(8,128)S(1)} %join.2.refs_4_.refs_0_), channel_id=1, source_target_pairs={{0,8},{4,12},{8,0},{12,4},{16,24},{20,28},{24,16},{28,20},{1,9},{5... | collective-permute-start | bytes 786440 | tf_op jit(solution)/shard_map/ppermute | solution.py:442
  17.8 8.9 %collective-permute-start.2 = (f32[64,256]{1,0:T(8,128)S(1)}, f32[64,256]{1,0:T(8,128)S(1)}, u32[]{:S(2)}, u32[]{:S(2)}) collective-permute-start(f32[64,256]{1,0:T(8,128)S(1)} %get-tuple-element.51), channel_id=1, source_target_pairs={{0,8},{4,12},{8,0},{12,4},{16,24},{20,28},{24,16},{28,20},{1,9},{5... | collective-permute-start | bytes 196616 | tf_op jit(solution)/shard_map/ppermute | solution.py:442
  19.4 7.3 %collective-permute-start.3 = (f32[64,256]{1,0:T(8,128)S(1)}, f32[64,256]{1,0:T(8,128)S(1)}, u32[]{:S(2)}, u32[]{:S(2)}) collective-permute-start(f32[64,256]{1,0:T(8,128)S(1)} %get-tuple-element.52), channel_id=1, source_target_pairs={{0,16},{4,20},{8,24},{12,28},{16,0},{20,4},{24,8},{28,12},{1,17},{... | collective-permute-start | bytes 196616 | tf_op jit(solution)/shard_map/ppermute | solution.py:442
  20.3 6.5 %collective-permute-start.4 = (f32[64,256]{1,0:T(8,128)S(1)}, f32[64,256]{1,0:T(8,128)S(1)}, u32[]{:S(2)}, u32[]{:S(2)}) collective-permute-start(f32[64,256]{1,0:T(8,128)S(1)} %get-tuple-element.53), channel_id=1, source_target_pairs={{0,24},{4,28},{8,16},{12,20},{16,8},{20,12},{24,0},{28,4},{1,25},{... | collective-permute-start | bytes 196616 | tf_op jit(solution)/shard_map/ppermute | solution.py:442
  26.7 6.6 %collective-permute-start.7 = (f32[64,256]{1,0:T(8,128)S(1)}, f32[64,256]{1,0:T(8,128)S(1)}, u32[]{:S(2)}, u32[]{:S(2)}) collective-permute-start(f32[64,256]{1,0:T(8,128)S(1)} %sum.1.refs_1_.refs_2_), channel_id=1, source_target_pairs={{0,24},{4,28},{8,16},{12,20},{16,8},{20,12},{24,0},{28,4},{1,25},{... | collective-permute-start | bytes 196616 | tf_op jit(solution)/shard_map/ppermute | solution.py:442
  29.5 5.2 %collective-permute-start.6 = (f32[64,256]{1,0:T(8,128)S(1)}, f32[64,256]{1,0:T(8,128)S(1)}, u32[]{:S(2)}, u32[]{:S(2)}) collective-permute-start(f32[64,256]{1,0:T(8,128)S(1)} %sum.1.refs_1_.refs_2_), channel_id=1, source_target_pairs={{0,16},{4,20},{8,24},{12,28},{16,0},{20,4},{24,8},{28,12},{1,17},{... | collective-permute-start | bytes 196616 | tf_op jit(solution)/shard_map/ppermute | solution.py:442
  29.5 5.2 %collective-permute-start.5 = (f32[64,256]{1,0:T(8,128)S(1)}, f32[64,256]{1,0:T(8,128)S(1)}, u32[]{:S(2)}, u32[]{:S(2)}) collective-permute-start(f32[64,256]{1,0:T(8,128)S(1)} %sum.1.refs_1_.refs_2_), channel_id=1, source_target_pairs={{0,8},{4,12},{8,0},{12,4},{16,24},{20,28},{24,16},{28,20},{1,9},{5... | collective-permute-start | bytes 196616 | tf_op jit(solution)/shard_map/ppermute | solution.py:442
  31.2 13.6 %collective-permute-start.12 = (f32[4,64,512]{2,1,0:T(8,128)S(1)}, f32[4,64,512]{2,1,0:T(8,128)S(1)}, u32[]{:S(2)}, u32[]{:S(2)}) collective-permute-start(f32[4,64,512]{2,1,0:T(8,128)S(1)} %join.3.refs_0_), channel_id=1, source_target_pairs={{0,4},{4,0},{8,12},{12,8},{16,20},{20,16},{24,28},{28,24},{1,5},{5... | collective-permute-start | bytes 1572872 | tf_op jit(solution)/shard_map/ppermute | solution.py:442
  35.3 7.4 %collective-permute-start.10 = (f32[64,128]{1,0:T(8,128)S(1)}, f32[64,128]{1,0:T(8,128)S(1)}, u32[]{:S(2)}, u32[]{:S(2)}) collective-permute-start(f32[64,128]{1,0:T(8,128)S(1)} %get-tuple-element.65.refs_3_), channel_id=1, source_target_pairs={{0,24},{4,28},{8,16},{12,20},{16,8},{20,12},{24,0},{28,4},{1,25},{... | collective-permute-start | bytes 98312 | tf_op jit(solution)/shard_map/ppermute | solution.py:442
  37.7 5.1 %collective-permute-start.9 = (f32[64,128]{1,0:T(8,128)S(1)}, f32[64,128]{1,0:T(8,128)S(1)}, u32[]{:S(2)}, u32[]{:S(2)}) collective-permute-start(f32[64,128]{1,0:T(8,128)S(1)} %get-tuple-element.65.refs_3_), channel_id=1, source_target_pairs={{0,16},{4,20},{8,24},{12,28},{16,0},{20,4},{24,8},{28,12},{1,17},{... | collective-permute-start | bytes 98312 | tf_op jit(solution)/shard_map/ppermute | solution.py:442
  37.7 5.1 %collective-permute-start.8 = (f32[64,128]{1,0:T(8,128)S(1)}, f32[64,128]{1,0:T(8,128)S(1)}, u32[]{:S(2)}, u32[]{:S(2)}) collective-permute-start(f32[64,128]{1,0:T(8,128)S(1)} %get-tuple-element.65.refs_3_), channel_id=1, source_target_pairs={{0,8},{4,12},{8,0},{12,4},{16,24},{20,28},{24,16},{28,20},{1,9},{5... | collective-permute-start | bytes 98312 | tf_op jit(solution)/shard_map/ppermute | solution.py:442
  42.9 5.4 %collective-permute-start.14 = (f32[64,640]{1,0:T(8,128)S(1)}, f32[64,640]{1,0:T(8,128)S(1)}, u32[]{:S(2)}, u32[]{:S(2)}) collective-permute-start(f32[64,640]{1,0:T(8,128)S(1)} %scaled.1.refs_2_.refs_9_), channel_id=1, source_target_pairs={{0,4},{4,0},{8,12},{12,8},{16,20},{20,16},{24,28},{28,24},{1,5},{5... | collective-permute-start | bytes 491528 | tf_op jit(solution)/shard_map/ppermute | solution.py:442
  44.8 3.5 %collective-permute-start.15 = (f32[4,64,512]{2,1,0:T(8,128)S(1)}, f32[4,64,512]{2,1,0:T(8,128)S(1)}, u32[]{:S(2)}, u32[]{:S(2)}) collective-permute-start(f32[4,64,512]{2,1,0:T(8,128)S(1)} %join.3.refs_0_), channel_id=1, source_target_pairs={{0,1},{1,0},{2,3},{3,2},{4,5},{5,4},{6,7},{7,6},{8,9},{9,8},{10,11... | collective-permute-start | bytes 1572872 | tf_op jit(solution)/shard_map/ppermute | solution.py:445
  44.8 3.5 %collective-permute-start.16 = (f32[4,64,512]{2,1,0:T(8,128)S(1)}, f32[4,64,512]{2,1,0:T(8,128)S(1)}, u32[]{:S(2)}, u32[]{:S(2)}) collective-permute-start(f32[4,64,512]{2,1,0:T(8,128)S(1)} %held.2.refs_3_.refs_1_), channel_id=1, source_target_pairs={{0,1},{1,0},{2,3},{3,2},{4,5},{5,4},{6,7},{7,6},{8,9},{9,8},{10,11... | collective-permute-start | bytes 1572872 | tf_op jit(solution)/shard_map/ppermute | solution.py:445
  46.0 8.3 %collective-permute-start.13 = (f32[64,1024]{1,0:T(8,128)S(1)}, f32[64,1024]{1,0:T(8,128)S(1)}, u32[]{:S(2)}, u32[]{:S(2)}) collective-permute-start(f32[64,1024]{1,0:T(8,128)S(1)} %spread.1.refs_4_), channel_id=1, source_target_pairs={{0,4},{4,0},{8,12},{12,8},{16,20},{20,16},{24,28},{28,24},{1,5},{5... | collective-permute-start | bytes 786440 | tf_op jit(solution)/shard_map/ppermute | solution.py:442
  50.4 1.5 %collective-permute-start.17 = (f32[64,640]{1,0:T(8,128)S(1)}, f32[64,640]{1,0:T(8,128)S(1)}, u32[]{:S(2)}, u32[]{:S(2)}) collective-permute-start(f32[64,640]{1,0:T(8,128)S(1)} %get-tuple-element.72.refs_0_.refs_1_), channel_id=1, source_target_pairs={{0,1},{1,0},{2,3},{3,2},{4,5},{5,4},{6,7},{7,6},{8,9},{9,8},{10,11... | collective-permute-start | bytes 491528 | tf_op jit(solution)/shard_map/ppermute | solution.py:445
  52.1 5.6 %collective-permute-start.18 = (f32[64,512]{1,0:T(8,128)S(1)}, f32[64,512]{1,0:T(8,128)S(1)}, u32[]{:S(2)}, u32[]{:S(2)}) collective-permute-start(f32[64,512]{1,0:T(8,128)S(1)} %slice.3), channel_id=1, source_target_pairs={{0,2},{1,3},{2,0},{3,1},{4,6},{5,7},{6,4},{7,5},{8,10},{9,11},{10,... | collective-permute-start | bytes 393224 | tf_op jit(solution)/shard_map/ppermute | solution.py:445
  (9 other events, 18.8 us)

commit v3 on v2

--- a/solution.py
+++ b/solution.py
@@ -391,16 +391,12 @@
     upper = lax.rem(lax.axis_index("row") // bit, 2) == 1
     prior = jnp.where(upper, other[...], carry[...])
     prior = dot3(near[:, width : width + rank], prior) + near[:, :width]
-    threes = []
-    for band in range(bands):
-        threes.append(stack3(prior))
-        prior = offsets[band] - dot3(gain[band][:, rank:], prior)
-        states[band] = prior
     copies = []
     for band in range(bands):
+        three = stack3(prior)
         for first, last in blocks_of(nb):
             solved[band, first:last, :] = (
-                partial[band, first:last, :] - bdot(feed[band][1, first:last, :], threes[band])
+                partial[band, first:last, :] - bdot(feed[band][1, first:last, :], three)
             ).astype(BF16)
             copy = pltpu.make_async_copy(
                 solved.at[band, first:last, :],
@@ -409,6 +405,8 @@
             )
             copy.start()
             copies.append(copy)
+        prior = offsets[band] - dot3(gain[band][:, rank:], prior)
+        states[band] = prior
     for copy in copies:
         copy.wait()
 
@@ -525,10 +523,10 @@
     if pieces > 1:
         (total,) = vmem_call(sum_body, [((rank, slab), F32)], name="sum")(
             parts[0],
-            *[swap(parts[step], 2 * step) for step in range(1, pieces)],
+            *[swap(parts[step], 2 * step) for step in reversed(range(1, pieces))],
             needs=(wide, matrix),
         )
-        slabs = [total] + [swap(total, 2 * step) for step in range(1, pieces)]
+        slabs = [total] + [swap(total, 2 * step) for step in reversed(range(1, pieces))][::-1]
     else:
         members = [list(range(side, cols, 2)) for side in range(2)]
         total = lax.psum(parts[0], "col", axis_index_groups=members)
@@ -543,7 +541,7 @@
         [((rank, nb), F32), ((rank, 2 * rank), F32), ((rank, rank), F32)],
         name="project",
     )(x_pair, *slabs)
-    crossed_all = [crossed] + [swap(crossed, 2 * step) for step in range(1, groups)]
+    crossed_all = [crossed] + [swap(crossed, 2 * step) for step in reversed(range(1, groups))][::-1]
     inverse_gram, upper, slope = vmem_call(
         functools.partial(factor_body, bands), [((rank, rank), F32)] * 3, flops=3 * 10**10, name="factor"
     )(gram, sketched, *right_rows)

time: 60.7 us -> 60.6 us (level)
  waiting for transfers between devices: 7.16 us -> 8.42 us
  starting transfers between devices: 27.8 us -> 26.6 us
    ppermute x15, starting transfers between devices: 25.7 us -> 24.4 us  [swap(): return lax.ppermute(x, 'col', [(c, c ^ step) for c in range(cols)])]
    ppermute x15, waiting for transfers between devices: 4.82 us -> 5.52 us  [swap(): return lax.ppermute(x, 'col', [(c, c ^ step) for c in range(cols)])]
  transfers between devices with their start and end apart: 19 -> 19, of which waited for: 7 -> 6; matrix products, arithmetic and copies ran while one was open for 6% -> 6% of each run, Pallas kernels for 28% -> 28%
where the time goes in v3:
time: 60.6 us; the launch traced here: 60.4 us
  starting transfers between devices  26.6 us (44%)
  Pallas kernels  19.5 us (32%)
  waiting for transfers between devices  8.42 us (14%)
  matrix products  3.76 us (6%)
  local copies, waits for them, and re-layouts  1.16 us (2%)
  between operations  0.97 us (2%)
    ppermute x15, starting transfers between devices, swap(): return lax.ppermute(x, 'col', [(c, c ^ step) for c in range(cols)])  24.4 us
    pallas_call x17, Pallas kernels, call(): pl.pallas_call(kernel, in_specs=[vmem] * count + [pl.BlockSpec(memory_spa...  14 us
    ppermute x15, waiting for transfers between devices, swap(): return lax.ppermute(x, 'col', [(c, c ^ step) for c in range(cols)])  5.52 us
    ppermute x4, waiting for transfers between devices, row_swap(): return lax.ppermute(x, 'row', [(r, r ^ step) for r in range(rows)])  2.9 us
    pallas_call x1, Pallas kernels, shards(): pl.pallas_call(couple_body, in_specs=hbm(5) + [pl.BlockSpec(memory_space=...  2.8 us
    pallas_call x1, Pallas kernels, shards(): pl.pallas_call(functools.partial(finish_body, bands, step), in_specs=[vme...  2.63 us
    dot_general x1, matrix products, shards(): jnp.dot(pivot_inverse, pivot_rhs, preferred_element_type=F32).astype(BF16)  2.47 us
    ppermute x4, starting transfers between devices, row_swap(): return lax.ppermute(x, 'row', [(r, r ^ step) for r in range(rows)])  2.18 us
  transfers between devices with their start and end apart: 19, of which 6 were waited for; matrix products, arithmetic and copies ran while one was open for 6% of the time, Pallas kernels for 28%

profile of v3, /device:TPU:0, one launch (start us, length us, event | category | flops | bytes accessed | tf_op | source)
XLA Modules:
  0.0 60.4 jit_solution(17443150353200364459)
XLA Ops:
  1.7 4.1 %collective-permute-start.1 = (f32[1,64,512]{2,1,0:T(8,128)S(1)}, f32[1,64,512]{2,1,0:T(8,128)S(1)}, u32[]{:S(2)}, u32[]{:S(2)}) collective-permute-start(f32[1,64,512]{2,1,0:T(8,128)S(1)} %widen.1.ready.refs_0_), channel_id=1, source_target_pairs={{0,16},{4,20},{8,24},{12,28},{16,0},{20,4},{24,8},{28,12},{1,17},{... | collective-permute-start | bytes 393224 | tf_op jit(solution)/shard_map/ppermute | solution.py:440
  5.8 2.8 %couple.1 = (f32[64,1024]{1,0:T(8,128)}, f32[64,1152]{1,0:T(8,128)}) custom-call(bf16[2,64,1024]{2,1,0:T(8,128)(2,1)} %bitcast.32, bf16[2,64,1024]{2,1,0:T(8,128)(2,1)} %bitcast.33, bf16[64,1024]{1,0:T(8,128)(2,1)} %bitcast.29, bf16[64,1024]{1,0:T(8,128)(2,1)} %bitcast.36, bf16[64,1024]{1,0:T(8,128)(2,1)} %bitcast.37, f32[1,64,512]{2,1,0:T(8,128)} %copy-done.3), custom_call_target="tpu_custom_call" | custom-call | tf_op jit(solution)/shard_map/couple/pallas_call | solution.py:459
  8.6 1.6 %collective-permute-start = (f32[64,1152]{1,0:T(8,128)}, f32[64,1152]{1,0:T(8,128)S(1)}, u32[]{:S(2)}, u32[]{:S(2)}) collective-permute-start(f32[64,1152]{1,0:T(8,128)} %get-tuple-element.43.refs_1_), channel_id=1, source_target_pairs={{0,4},{4,0},{8,12},{12,8},{16,20},{20,16},{24,28},{28,24},{1,5},{5... | collective-permute-start | bytes 884744 | tf_op jit(solution)/shard_map/ppermute | solution.py:440
  10.2 2.5 %convolution_convert_fusion = bf16[1024,512]{1,0:T(8,128)(2,1)S(1)} fusion(bf16[1024,1024]{1,0:T(8,128)(2,1)S(1)} %copy-done, bf16[1024,512]{1,0:T(8,128)(2,1)} %param.25), kind=kOutput, calls=%fused_computation.1 | convolution fusion | flops 1074266112 | bytes 4194304 | tf_op jit(solution)/shard_map/dot_general | solution.py:486
  14.2 1.6 %collective-permute-start.11 = (f32[2,64,512]{2,1,0:T(8,128)S(1)}, f32[2,64,512]{2,1,0:T(8,128)S(1)}, u32[]{:S(2)}, u32[]{:S(2)}) collective-permute-start(f32[2,64,512]{2,1,0:T(8,128)S(1)} %join.2.refs_4_.refs_0_), channel_id=1, source_target_pairs={{0,8},{4,12},{8,0},{12,4},{16,24},{20,28},{24,16},{28,20},{1,9},{5... | collective-permute-start | bytes 786440 | tf_op jit(solution)/shard_map/ppermute | solution.py:440
  15.9 1.5 %collective-permute-done.refs_2_ = f32[64,1152]{1,0:T(8,128)S(1)} collective-permute-done((f32[64,1152]{1,0:T(8,128)}, f32[64,1152]{1,0:T(8,128)S(1)}, u32[]{:S(2)}, u32[]{:S(2)}) %collective-permute-start) | collective-permute-done | bytes 294944 | tf_op jit(solution)/shard_map/ppermute | solution.py:440
  17.8 1.9 %collective-permute-start.2 = (f32[64,256]{1,0:T(8,128)S(1)}, f32[64,256]{1,0:T(8,128)S(1)}, u32[]{:S(2)}, u32[]{:S(2)}) collective-permute-start(f32[64,256]{1,0:T(8,128)S(1)} %get-tuple-element.51), channel_id=1, source_target_pairs={{0,24},{4,28},{8,16},{12,20},{16,8},{20,12},{24,0},{28,4},{1,25},{... | collective-permute-start | bytes 196616 | tf_op jit(solution)/shard_map/ppermute | solution.py:440
  20.9 1.3 %collective-permute-start.4 = (f32[64,256]{1,0:T(8,128)S(1)}, f32[64,256]{1,0:T(8,128)S(1)}, u32[]{:S(2)}, u32[]{:S(2)}) collective-permute-start(f32[64,256]{1,0:T(8,128)S(1)} %get-tuple-element.53), channel_id=1, source_target_pairs={{0,8},{4,12},{8,0},{12,4},{16,24},{20,28},{24,16},{28,20},{1,9},{5... | collective-permute-start | bytes 196616 | tf_op jit(solution)/shard_map/ppermute | solution.py:440
  22.2 1.6 %band.2 = (f32[1024,512]{1,0:T(8,128)S(1)}, bf16[2,1024,192]{2,1,0:T(8,128)(2,1)S(1)}, f32[64,512]{1,0:T(8,128)S(1)}, f32[64,128]{1,0:T(8,128)S(1)}, f32[64,1024]{1,0:T(8,128)S(1)}) custom-call(bf16[2,1024,1024]{2,1,0:T(8,128)(2,1)S(1)} %copy-done.1, bf16[2,1024,512]{2,1,0:T(8,128)(2,1)S(1)} %copy-done.2, bf16[2,128,1024]{2,1,0:T(8,128)(2,1)S(1)} %pad_maximum_fusion.refs_2_, ...), custom_call_target="tpu_custom_call" | custom-call | flops 2000000000 | bytes 1000000 | tf_op jit(solution)/shard_map/band/pallas_call | solution.py:47
  23.9 1.6 %band.3 = (f32[1024,512]{1,0:T(8,128)S(1)}, bf16[2,1024,192]{2,1,0:T(8,128)(2,1)S(1)}, f32[64,512]{1,0:T(8,128)S(1)}, f32[64,128]{1,0:T(8,128)S(1)}, f32[64,1024]{1,0:T(8,128)S(1)}) custom-call(bf16[2,1024,1024]{2,1,0:T(8,128)(2,1)S(1)} %copy-done.1, bf16[2,1024,512]{2,1,0:T(8,128)(2,1)S(1)} %copy-done.2, bf16[2,128,1024]{2,1,0:T(8,128)(2,1)S(1)} %pad_maximum_fusion.refs_2_, ...), custom_call_target="tpu_custom_call" | custom-call | flops 2000000000 | bytes 1000000 | tf_op jit(solution)/shard_map/band/pallas_call | solution.py:47
  26.7 1.9 %collective-permute-start.7 = (f32[64,256]{1,0:T(8,128)S(1)}, f32[64,256]{1,0:T(8,128)S(1)}, u32[]{:S(2)}, u32[]{:S(2)}) collective-permute-start(f32[64,256]{1,0:T(8,128)S(1)} %sum.1.refs_1_.refs_2_), channel_id=1, source_target_pairs={{0,24},{4,28},{8,16},{12,20},{16,8},{20,12},{24,0},{28,4},{1,25},{... | collective-permute-start | bytes 196616 | tf_op jit(solution)/shard_map/ppermute | solution.py:440
  29.1 2.1 %collective-permute-start.5 = (f32[64,256]{1,0:T(8,128)S(1)}, f32[64,256]{1,0:T(8,128)S(1)}, u32[]{:S(2)}, u32[]{:S(2)}) collective-permute-start(f32[64,256]{1,0:T(8,128)S(1)} %sum.1.refs_1_.refs_2_), channel_id=1, source_target_pairs={{0,8},{4,12},{8,0},{12,4},{16,24},{20,28},{24,16},{28,20},{1,9},{5... | collective-permute-start | bytes 196616 | tf_op jit(solution)/shard_map/ppermute | solution.py:440
  31.2 1.6 %collective-permute-start.12 = (f32[4,64,512]{2,1,0:T(8,128)S(1)}, f32[4,64,512]{2,1,0:T(8,128)S(1)}, u32[]{:S(2)}, u32[]{:S(2)}) collective-permute-start(f32[4,64,512]{2,1,0:T(8,128)S(1)} %join.3.refs_0_), channel_id=1, source_target_pairs={{0,4},{4,0},{8,12},{12,8},{16,20},{20,16},{24,28},{28,24},{1,5},{5... | collective-permute-start | bytes 1572872 | tf_op jit(solution)/shard_map/ppermute | solution.py:440
  32.9 1.4 %collective-permute-done.6.refs_3_ = f32[64,256]{1,0:T(8,128)S(1)} collective-permute-done((f32[64,256]{1,0:T(8,128)S(1)}, f32[64,256]{1,0:T(8,128)S(1)}, u32[]{:S(2)}, u32[]{:S(2)}) %collective-permute-start.6) | collective-permute-done | bytes 65568 | tf_op jit(solution)/shard_map/ppermute | solution.py:440
  34.9 2.0 %collective-permute-start.10 = (f32[64,128]{1,0:T(8,128)S(1)}, f32[64,128]{1,0:T(8,128)S(1)}, u32[]{:S(2)}, u32[]{:S(2)}) collective-permute-start(f32[64,128]{1,0:T(8,128)S(1)} %get-tuple-element.65.refs_3_), channel_id=1, source_target_pairs={{0,24},{4,28},{8,16},{12,20},{16,8},{20,12},{24,0},{28,4},{1,25},{... | collective-permute-start | bytes 98312 | tf_op jit(solution)/shard_map/ppermute | solution.py:440
  37.6 1.7 %collective-permute-start.8 = (f32[64,128]{1,0:T(8,128)S(1)}, f32[64,128]{1,0:T(8,128)S(1)}, u32[]{:S(2)}, u32[]{:S(2)}) collective-permute-start(f32[64,128]{1,0:T(8,128)S(1)} %get-tuple-element.65.refs_3_), channel_id=1, source_target_pairs={{0,8},{4,12},{8,0},{12,4},{16,24},{20,28},{24,16},{28,20},{1,9},{5... | collective-permute-start | bytes 98312 | tf_op jit(solution)/shard_map/ppermute | solution.py:440
  39.4 2.9 %factor.1 = (f32[64,64]{1,0:T(8,128)S(1)}, f32[64,64]{1,0:T(8,128)S(1)}, f32[64,64]{1,0:T(8,128)S(1)}) custom-call(f32[64,64]{1,0:T(8,128)S(1)} %get-tuple-element.60.refs_0_, f32[64,1024]{1,0:T(8,128)S(1)} %get-tuple-element.59.refs_1_, f32[64,1024]{1,0:T(8,128)S(1)} %get-tuple-element.46.refs_5_.refs_2_, f32[64,1024]{1,0:T(8,128)S(1)} %get-tuple-element.61.refs_3_), custom_call_target="tpu_custom_call" | custom-call | flops 30000001024 | bytes 1000000 | tf_op jit(solution)/shard_map/factor/pallas_call | solution.py:47
  42.5 1.8 %collective-permute-start.14 = (f32[64,640]{1,0:T(8,128)S(1)}, f32[64,640]{1,0:T(8,128)S(1)}, u32[]{:S(2)}, u32[]{:S(2)}) collective-permute-start(f32[64,640]{1,0:T(8,128)S(1)} %scaled.1.refs_2_.refs_9_), channel_id=1, source_target_pairs={{0,4},{4,0},{8,12},{12,8},{16,20},{20,16},{24,28},{28,24},{1,5},{5... | collective-permute-start | bytes 491528 | tf_op jit(solution)/shard_map/ppermute | solution.py:440
  45.8 2.5 %collective-permute-done.14.refs_0_ = f32[64,640]{1,0:T(8,128)S(1)} collective-permute-done((f32[64,640]{1,0:T(8,128)S(1)}, f32[64,640]{1,0:T(8,128)S(1)}, u32[]{:S(2)}, u32[]{:S(2)}) %collective-permute-start.14) | collective-permute-done | bytes 163872 | tf_op jit(solution)/shard_map/ppermute | solution.py:440
  50.5 1.4 %collective-permute-done.17.refs_2_ = f32[64,640]{1,0:T(8,128)S(1)} collective-permute-done((f32[64,640]{1,0:T(8,128)S(1)}, f32[64,640]{1,0:T(8,128)S(1)}, u32[]{:S(2)}, u32[]{:S(2)}) %collective-permute-start.17) | collective-permute-done | bytes 163872 | tf_op jit(solution)/shard_map/ppermute | solution.py:443
  52.1 1.6 %collective-permute-start.18 = (f32[64,512]{1,0:T(8,128)S(1)}, f32[64,512]{1,0:T(8,128)S(1)}, u32[]{:S(2)}, u32[]{:S(2)}) collective-permute-start(f32[64,512]{1,0:T(8,128)S(1)} %slice.3), channel_id=1, source_target_pairs={{0,2},{1,3},{2,0},{3,1},{4,6},{5,7},{6,4},{7,5},{8,10},{9,11},{10,... | collective-permute-start | bytes 393224 | tf_op jit(solution)/shard_map/ppermute | solution.py:443
  53.7 2.5 %partial.1 = (f32[2,1024,512]{2,1,0:T(8,128)S(1)}, f32[2,64,512]{2,1,0:T(8,128)S(1)}, f32[2,64,128]{2,1,0:T(8,128)}) custom-call(f32[1024,512]{1,0:T(8,128)S(1)} %get-tuple-element.45.refs_0_, f32[1024,512]{1,0:T(8,128)S(1)} %get-tuple-element.47.refs_1_, bf16[2,1024,192]{2,1,0:T(8,128)(2,1)S(1)} %get-tuple-element.48.refs_2_.refs_0_, ...), custom_call_target="tpu_custom_call" | custom-call | flops 1000000000 | bytes 1000000 | tf_op jit(solution)/shard_map/partial/pallas_call | solution.py:47
  56.2 1.5 %collective-permute-done.18.refs_7_ = f32[64,512]{1,0:T(8,128)S(1)} collective-permute-done((f32[64,512]{1,0:T(8,128)S(1)}, f32[64,512]{1,0:T(8,128)S(1)}, u32[]{:S(2)}, u32[]{:S(2)}) %collective-permute-start.18) | collective-permute-done | bytes 131104 | tf_op jit(solution)/shard_map/ppermute | solution.py:443
  57.8 2.6 %finish.1 = (bf16[2,1024,512]{2,1,0:T(8,128)(2,1)}, f32[2,64,512]{2,1,0:T(8,128)}) custom-call(bf16[2,1024,192]{2,1,0:T(8,128)(2,1)S(1)} %get-tuple-element.48.refs_2_.refs_0_, bf16[2,1024,192]{2,1,0:T(8,128)(2,1)S(1)} %get-tuple-element.49.refs_3_.refs_1_, f32[64,128]{1,0:T(8,128)S(1)} %get-tuple-element.56.refs_2_.refs_0_, ...), custom_call_target="tpu_custom_call" | custom-call | flops 1000000000 | bytes 1000000 | tf_op jit(solution)/shard_map/finish/pallas_call | solution.py:607
  (67 shorter events, 11.2 us)
Async XLA Ops:
  0.6 9.6 %copy-start = (bf16[1024,1024]{1,0:T(8,128)(2,1)S(1)}, bf16[1024,1024]{1,0:T(8,128)(2,1)}, u32[]{:S(2)}) copy-start(bf16[1024,1024]{1,0:T(8,128)(2,1)} %param.21) | copy-start | bytes 6291460
  1.7 12.4 %collective-permute-start.1 = (f32[1,64,512]{2,1,0:T(8,128)S(1)}, f32[1,64,512]{2,1,0:T(8,128)S(1)}, u32[]{:S(2)}, u32[]{:S(2)}) collective-permute-start(f32[1,64,512]{2,1,0:T(8,128)S(1)} %widen.1.ready.refs_0_), channel_id=1, source_target_pairs={{0,16},{4,20},{8,24},{12,28},{16,0},{20,4},{24,8},{28,12},{1,17},{... | collective-permute-start | bytes 393224 | tf_op jit(solution)/shard_map/ppermute | solution.py:440
  8.6 8.7 %collective-permute-start = (f32[64,1152]{1,0:T(8,128)}, f32[64,1152]{1,0:T(8,128)S(1)}, u32[]{:S(2)}, u32[]{:S(2)}) collective-permute-start(f32[64,1152]{1,0:T(8,128)} %get-tuple-element.43.refs_1_), channel_id=1, source_target_pairs={{0,4},{4,0},{8,12},{12,8},{16,20},{20,16},{24,28},{28,24},{1,5},{5... | collective-permute-start | bytes 884744 | tf_op jit(solution)/shard_map/ppermute | solution.py:440
  12.7 4.6 %copy-start.8 = (f32[64,1152]{1,0:T(8,128)S(1)}, f32[64,1152]{1,0:T(8,128)}, u32[]{:S(2)}) copy-start(f32[64,1152]{1,0:T(8,128)} %get-tuple-element.43.refs_1_) | copy-start | bytes 884740
  12.8 9.5 %copy-start.2 = (bf16[2,1024,512]{2,1,0:T(8,128)(2,1)S(1)}, bf16[2,1024,512]{2,1,0:T(8,128)(2,1)}, u32[]{:S(2)}) copy-start(bf16[2,1024,512]{2,1,0:T(8,128)(2,1)} %refs_1_.3) | copy-start | bytes 6291460
  14.1 8.1 %copy-start.1 = (bf16[2,1024,1024]{2,1,0:T(8,128)(2,1)S(1)}, bf16[2,1024,1024]{2,1,0:T(8,128)(2,1)}, u32[]{:S(2)}) copy-start(bf16[2,1024,1024]{2,1,0:T(8,128)(2,1)} %refs_0_.5) | copy-start | bytes 12582916
  14.2 8.1 %copy-start.5 = (bf16[2,1024,64]{1,2,0:T(8,128)(2,1)S(1)}, bf16[2,1024,64]{1,2,0:T(8,128)(2,1)}, u32[]{:S(2)}) copy-start(bf16[2,1024,64]{1,2,0:T(8,128)(2,1)} %param.24) | copy-start | bytes 786436
  14.2 17.0 %collective-permute-start.11 = (f32[2,64,512]{2,1,0:T(8,128)S(1)}, f32[2,64,512]{2,1,0:T(8,128)S(1)}, u32[]{:S(2)}, u32[]{:S(2)}) collective-permute-start(f32[2,64,512]{2,1,0:T(8,128)S(1)} %join.2.refs_4_.refs_0_), channel_id=1, source_target_pairs={{0,8},{4,12},{8,0},{12,4},{16,24},{20,28},{24,16},{28,20},{1,9},{5... | collective-permute-start | bytes 786440 | tf_op jit(solution)/shard_map/ppermute | solution.py:440
  17.8 8.9 %collective-permute-start.2 = (f32[64,256]{1,0:T(8,128)S(1)}, f32[64,256]{1,0:T(8,128)S(1)}, u32[]{:S(2)}, u32[]{:S(2)}) collective-permute-start(f32[64,256]{1,0:T(8,128)S(1)} %get-tuple-element.51), channel_id=1, source_target_pairs={{0,24},{4,28},{8,16},{12,20},{16,8},{20,12},{24,0},{28,4},{1,25},{... | collective-permute-start | bytes 196616 | tf_op jit(solution)/shard_map/ppermute | solution.py:440
  19.7 7.0 %collective-permute-start.3 = (f32[64,256]{1,0:T(8,128)S(1)}, f32[64,256]{1,0:T(8,128)S(1)}, u32[]{:S(2)}, u32[]{:S(2)}) collective-permute-start(f32[64,256]{1,0:T(8,128)S(1)} %get-tuple-element.52), channel_id=1, source_target_pairs={{0,16},{4,20},{8,24},{12,28},{16,0},{20,4},{24,8},{28,12},{1,17},{... | collective-permute-start | bytes 196616 | tf_op jit(solution)/shard_map/ppermute | solution.py:440
  20.9 5.8 %collective-permute-start.4 = (f32[64,256]{1,0:T(8,128)S(1)}, f32[64,256]{1,0:T(8,128)S(1)}, u32[]{:S(2)}, u32[]{:S(2)}) collective-permute-start(f32[64,256]{1,0:T(8,128)S(1)} %get-tuple-element.53), channel_id=1, source_target_pairs={{0,8},{4,12},{8,0},{12,4},{16,24},{20,28},{24,16},{28,20},{1,9},{5... | collective-permute-start | bytes 196616 | tf_op jit(solution)/shard_map/ppermute | solution.py:440
  26.7 6.1 %collective-permute-start.7 = (f32[64,256]{1,0:T(8,128)S(1)}, f32[64,256]{1,0:T(8,128)S(1)}, u32[]{:S(2)}, u32[]{:S(2)}) collective-permute-start(f32[64,256]{1,0:T(8,128)S(1)} %sum.1.refs_1_.refs_2_), channel_id=1, source_target_pairs={{0,24},{4,28},{8,16},{12,20},{16,8},{20,12},{24,0},{28,4},{1,25},{... | collective-permute-start | bytes 196616 | tf_op jit(solution)/shard_map/ppermute | solution.py:440
  28.7 5.6 %collective-permute-start.6 = (f32[64,256]{1,0:T(8,128)S(1)}, f32[64,256]{1,0:T(8,128)S(1)}, u32[]{:S(2)}, u32[]{:S(2)}) collective-permute-start(f32[64,256]{1,0:T(8,128)S(1)} %sum.1.refs_1_.refs_2_), channel_id=1, source_target_pairs={{0,16},{4,20},{8,24},{12,28},{16,0},{20,4},{24,8},{28,12},{1,17},{... | collective-permute-start | bytes 196616 | tf_op jit(solution)/shard_map/ppermute | solution.py:440
  29.1 5.2 %collective-permute-start.5 = (f32[64,256]{1,0:T(8,128)S(1)}, f32[64,256]{1,0:T(8,128)S(1)}, u32[]{:S(2)}, u32[]{:S(2)}) collective-permute-start(f32[64,256]{1,0:T(8,128)S(1)} %sum.1.refs_1_.refs_2_), channel_id=1, source_target_pairs={{0,8},{4,12},{8,0},{12,4},{16,24},{20,28},{24,16},{28,20},{1,9},{5... | collective-permute-start | bytes 196616 | tf_op jit(solution)/shard_map/ppermute | solution.py:440
  31.2 13.0 %collective-permute-start.12 = (f32[4,64,512]{2,1,0:T(8,128)S(1)}, f32[4,64,512]{2,1,0:T(8,128)S(1)}, u32[]{:S(2)}, u32[]{:S(2)}) collective-permute-start(f32[4,64,512]{2,1,0:T(8,128)S(1)} %join.3.refs_0_), channel_id=1, source_target_pairs={{0,4},{4,0},{8,12},{12,8},{16,20},{20,16},{24,28},{28,24},{1,5},{5... | collective-permute-start | bytes 1572872 | tf_op jit(solution)/shard_map/ppermute | solution.py:440
  34.9 7.4 %collective-permute-start.10 = (f32[64,128]{1,0:T(8,128)S(1)}, f32[64,128]{1,0:T(8,128)S(1)}, u32[]{:S(2)}, u32[]{:S(2)}) collective-permute-start(f32[64,128]{1,0:T(8,128)S(1)} %get-tuple-element.65.refs_3_), channel_id=1, source_target_pairs={{0,24},{4,28},{8,16},{12,20},{16,8},{20,12},{24,0},{28,4},{1,25},{... | collective-permute-start | bytes 98312 | tf_op jit(solution)/shard_map/ppermute | solution.py:440
  36.9 5.4 %collective-permute-start.9 = (f32[64,128]{1,0:T(8,128)S(1)}, f32[64,128]{1,0:T(8,128)S(1)}, u32[]{:S(2)}, u32[]{:S(2)}) collective-permute-start(f32[64,128]{1,0:T(8,128)S(1)} %get-tuple-element.65.refs_3_), channel_id=1, source_target_pairs={{0,16},{4,20},{8,24},{12,28},{16,0},{20,4},{24,8},{28,12},{1,17},{... | collective-permute-start | bytes 98312 | tf_op jit(solution)/shard_map/ppermute | solution.py:440
  37.6 4.7 %collective-permute-start.8 = (f32[64,128]{1,0:T(8,128)S(1)}, f32[64,128]{1,0:T(8,128)S(1)}, u32[]{:S(2)}, u32[]{:S(2)}) collective-permute-start(f32[64,128]{1,0:T(8,128)S(1)} %get-tuple-element.65.refs_3_), channel_id=1, source_target_pairs={{0,8},{4,12},{8,0},{12,4},{16,24},{20,28},{24,16},{28,20},{1,9},{5... | collective-permute-start | bytes 98312 | tf_op jit(solution)/shard_map/ppermute | solution.py:440
  42.5 5.8 %collective-permute-start.14 = (f32[64,640]{1,0:T(8,128)S(1)}, f32[64,640]{1,0:T(8,128)S(1)}, u32[]{:S(2)}, u32[]{:S(2)}) collective-permute-start(f32[64,640]{1,0:T(8,128)S(1)} %scaled.1.refs_2_.refs_9_), channel_id=1, source_target_pairs={{0,4},{4,0},{8,12},{12,8},{16,20},{20,16},{24,28},{28,24},{1,5},{5... | collective-permute-start | bytes 491528 | tf_op jit(solution)/shard_map/ppermute | solution.py:440
  44.3 4.1 %collective-permute-start.15 = (f32[4,64,512]{2,1,0:T(8,128)S(1)}, f32[4,64,512]{2,1,0:T(8,128)S(1)}, u32[]{:S(2)}, u32[]{:S(2)}) collective-permute-start(f32[4,64,512]{2,1,0:T(8,128)S(1)} %join.3.refs_0_), channel_id=1, source_target_pairs={{0,1},{1,0},{2,3},{3,2},{4,5},{5,4},{6,7},{7,6},{8,9},{9,8},{10,11... | collective-permute-start | bytes 1572872 | tf_op jit(solution)/shard_map/ppermute | solution.py:443
  44.3 4.1 %collective-permute-start.16 = (f32[4,64,512]{2,1,0:T(8,128)S(1)}, f32[4,64,512]{2,1,0:T(8,128)S(1)}, u32[]{:S(2)}, u32[]{:S(2)}) collective-permute-start(f32[4,64,512]{2,1,0:T(8,128)S(1)} %held.2.refs_3_.refs_1_), channel_id=1, source_target_pairs={{0,1},{1,0},{2,3},{3,2},{4,5},{5,4},{6,7},{7,6},{8,9},{9,8},{10,11... | collective-permute-start | bytes 1572872 | tf_op jit(solution)/shard_map/ppermute | solution.py:443
  45.4 8.3 %collective-permute-start.13 = (f32[64,1024]{1,0:T(8,128)S(1)}, f32[64,1024]{1,0:T(8,128)S(1)}, u32[]{:S(2)}, u32[]{:S(2)}) collective-permute-start(f32[64,1024]{1,0:T(8,128)S(1)} %spread.1.refs_4_), channel_id=1, source_target_pairs={{0,4},{4,0},{8,12},{12,8},{16,20},{20,16},{24,28},{28,24},{1,5},{5... | collective-permute-start | bytes 786440 | tf_op jit(solution)/shard_map/ppermute | solution.py:440
  50.4 1.5 %collective-permute-start.17 = (f32[64,640]{1,0:T(8,128)S(1)}, f32[64,640]{1,0:T(8,128)S(1)}, u32[]{:S(2)}, u32[]{:S(2)}) collective-permute-start(f32[64,640]{1,0:T(8,128)S(1)} %get-tuple-element.72.refs_0_.refs_1_), channel_id=1, source_target_pairs={{0,1},{1,0},{2,3},{3,2},{4,5},{5,4},{6,7},{7,6},{8,9},{9,8},{10,11... | collective-permute-start | bytes 491528 | tf_op jit(solution)/shard_map/ppermute | solution.py:443
  52.1 5.6 %collective-permute-start.18 = (f32[64,512]{1,0:T(8,128)S(1)}, f32[64,512]{1,0:T(8,128)S(1)}, u32[]{:S(2)}, u32[]{:S(2)}) collective-permute-start(f32[64,512]{1,0:T(8,128)S(1)} %slice.3), channel_id=1, source_target_pairs={{0,2},{1,3},{2,0},{3,1},{4,6},{5,7},{6,4},{7,5},{8,10},{9,11},{10,... | collective-permute-start | bytes 393224 | tf_op jit(solution)/shard_map/ppermute | solution.py:443
  (9 other events, 18.8 us)

commit v4 on v3

--- a/solution.py
+++ b/solution.py
@@ -182,16 +182,6 @@
             for row in range(chunk.shape[0]):
                 out[order[index], side, :, pl.ds(start, half)] = chunk[row].astype(BF16)
                 index += 1
-
-
-def wide_pulled_body(wide, pulled, high_out, low_out):
-    pulled_high, pulled_low = halves(pulled[...])
-    for first, last in blocks_of(wide.shape[0]):
-        rows = wide[first:last, :]
-        product = bdot(rows, pulled_high) + bdot(rows, pulled_low)
-        high, low = halves(product)
-        high_out[first:last, :] = high
-        low_out[first:last, :] = low
 
 
 def factor_body(bands, gram, sketched, *refs):
@@ -277,10 +267,13 @@
 
 def affine_body(bands, *refs):
     offset, gain = refs[:bands], refs[bands : 2 * bands]
-    panel_right, pulled, carry, coeffs, plain, constant, matrix_out = refs[2 * bands :]
+    panel_right, pulled, carry, coeffs, plain, constant, matrix_out, high_out, low_out = refs[2 * bands :]
     rank = carry.shape[0]
     stacked = jnp.concatenate([panel_right[band] for band in range(bands)], 0)
-    both = dot2(stacked, pulled[...])
+    high, low = halves(pulled[...])
+    high_out[...] = high
+    low_out[...] = low
+    both = bdot(stacked, high) + bdot(stacked, low)
     for band in range(bands):
         coeffs[band] = both[band * rank : (band + 1) * rank]
     constant_now = None
@@ -303,14 +296,17 @@
 
 def weight_body(bands, *refs):
     gain = refs[:bands]
-    own, other, wp_high, wp_low, constant, matrix, weights, pack = refs[bands:]
+    own, other, wide, pulled_high, pulled_low, constant, matrix, weights, pack = refs[bands:]
     parity = lax.rem(lax.axis_index("col"), 2)
     rank = own.shape[0]
-    count, width = wp_high.shape
+    count = wide.shape[0]
+    width = pulled_high.shape[1]
     sides = [middle[:, :count] for middle in (own, other)]
     highs, lows = zip(*[halves(side) for side in sides])
-    upper = bdot(jnp.concatenate(highs + lows, 0), wp_high[...])
-    lower = bdot(jnp.concatenate(highs, 0), wp_low[...])
+    both = bdot(jnp.concatenate(highs + lows, 0), wide[...])
+    high, low = halves(both[: bands * rank] + both[bands * rank :])
+    upper = bdot(jnp.concatenate([high, low], 0), pulled_high[...])
+    lower = bdot(high, pulled_low[...])
     own_first = upper[: bands * rank] + (upper[bands * rank :] + lower)
     own_weight, other_weight = own_first[:rank], own_first[rank:]
     ordered = []
@@ -514,9 +510,11 @@
     for band in range(bands):
         whole_bands.append(one_band(band, x_pair, *(last[-1] for last in whole_bands[-1:])))
     bases, feeds, offsets_in, gains, right_rows = zip(*whole_bands)
-    coeffs, plain, constant, matrix = vmem_call(
+    coeffs, plain, constant, matrix, pulled_high, pulled_low = vmem_call(
         functools.partial(affine_body, bands),
-        [((bands, rank, width), F32)] * 2 + [((rank, width), F32), ((rank, rank), F32)],
+        [((bands, rank, width), F32)] * 2
+        + [((rank, width), F32), ((rank, rank), F32)]
+        + [((nb, width), BF16)] * 2,
         name="affine",
     )(*offsets_in, *gains, turned(panel_right), pulled, carry_in)
 
@@ -558,14 +556,11 @@
         functools.partial(narrow_body, order), [((groups, 2, rank, nb), BF16)], name="narrow"
     )(wide, wide_other, row_swap(wide, 1), row_swap(wide_other, 1))
     wide = wide.reshape(count, nb)
-    wp_high, wp_low = vmem_call(
-        wide_pulled_body, [((count, width), BF16)] * 2, name="wide_pulled"
-    )(wide, pulled)
     weights, pack = vmem_call(
         functools.partial(weight_body, bands),
         [((bands, rank, width), F32), ((rank, width + LANES), F32)],
         name="weight",
-    )(*gains, middle, middle_other, wp_high, wp_low, constant, matrix)
+    )(*gains, middle, middle_other, wide, pulled_high, pulled_low, constant, matrix)
 
     near, group = pack, pack
     step = 1

time: 60.6 us -> 59.6 us (0.983)
  Pallas kernels: 19.5 us -> 18.7 us
    ppermute x4, waiting for transfers between devices: 2.9 us -> 1.94 us  [row_swap(): return lax.ppermute(x, 'row', [(r, r ^ step) for r in range(rows)])]
    pallas_call x17 -> x16, Pallas kernels: 14 us -> 13.3 us  [call(): pl.pallas_call(kernel, in_specs=[vmem] * count + [pl.BlockSpec(memory_spa...]
  transfers between devices with their start and end apart: 19 -> 19, of which waited for: 6 -> 7; matrix products, arithmetic and copies ran while one was open for 6% -> 6% of each run, Pallas kernels for 28% -> 27%
where the time goes in v4:
time: 59.6 us; the launch traced here: 59.4 us
  starting transfers between devices  26.7 us (45%)
  Pallas kernels  18.7 us (31%)
  waiting for transfers between devices  8.01 us (13%)
  matrix products  3.76 us (6%)
  local copies, waits for them, and re-layouts  1.16 us (2%)
  between operations  0.96 us (2%)
    ppermute x15, starting transfers between devices, swap(): return lax.ppermute(x, 'col', [(c, c ^ step) for c in range(cols)])  24.4 us
    pallas_call x16, Pallas kernels, call(): pl.pallas_call(kernel, in_specs=[vmem] * count + [pl.BlockSpec(memory_spa...  13.3 us
    ppermute x15, waiting for transfers between devices, swap(): return lax.ppermute(x, 'col', [(c, c ^ step) for c in range(cols)])  6.08 us
    pallas_call x1, Pallas kernels, shards(): pl.pallas_call(couple_body, in_specs=hbm(5) + [pl.BlockSpec(memory_space=...  2.8 us
    pallas_call x1, Pallas kernels, shards(): pl.pallas_call(functools.partial(finish_body, bands, step), in_specs=[vme...  2.63 us
    dot_general x1, matrix products, shards(): jnp.dot(pivot_inverse, pivot_rhs, preferred_element_type=F32).astype(BF16)  2.47 us
    ppermute x4, starting transfers between devices, row_swap(): return lax.ppermute(x, 'row', [(r, r ^ step) for r in range(rows)])  2.3 us
    ppermute x4, waiting for transfers between devices, row_swap(): return lax.ppermute(x, 'row', [(r, r ^ step) for r in range(rows)])  1.94 us
  transfers between devices with their start and end apart: 19, of which 7 were waited for; matrix products, arithmetic and copies ran while one was open for 6% of the time, Pallas kernels for 27%

profile of v4, /device:TPU:0, one launch (start us, length us, event | category | flops | bytes accessed | tf_op | source)
XLA Modules:
  0.0 59.4 jit_solution(14702028130968331244)
XLA Ops:
  1.7 4.1 %collective-permute-start.1 = (f32[1,64,512]{2,1,0:T(8,128)S(1)}, f32[1,64,512]{2,1,0:T(8,128)S(1)}, u32[]{:S(2)}, u32[]{:S(2)}) collective-permute-start(f32[1,64,512]{2,1,0:T(8,128)S(1)} %widen.1.ready.refs_0_), channel_id=1, source_target_pairs={{0,16},{4,20},{8,24},{12,28},{16,0},{20,4},{24,8},{28,12},{1,17},{... | collective-permute-start | bytes 393224 | tf_op jit(solution)/shard_map/ppermute | solution.py:436
  5.8 2.8 %couple.1 = (f32[64,1024]{1,0:T(8,128)}, f32[64,1152]{1,0:T(8,128)}) custom-call(bf16[2,64,1024]{2,1,0:T(8,128)(2,1)} %bitcast.32, bf16[2,64,1024]{2,1,0:T(8,128)(2,1)} %bitcast.33, bf16[64,1024]{1,0:T(8,128)(2,1)} %bitcast.29, bf16[64,1024]{1,0:T(8,128)(2,1)} %bitcast.36, bf16[64,1024]{1,0:T(8,128)(2,1)} %bitcast.37, f32[1,64,512]{2,1,0:T(8,128)} %copy-done.3), custom_call_target="tpu_custom_call" | custom-call | tf_op jit(solution)/shard_map/couple/pallas_call | solution.py:455
  8.6 1.6 %collective-permute-start = (f32[64,1152]{1,0:T(8,128)}, f32[64,1152]{1,0:T(8,128)S(1)}, u32[]{:S(2)}, u32[]{:S(2)}) collective-permute-start(f32[64,1152]{1,0:T(8,128)} %get-tuple-element.43.refs_1_), channel_id=1, source_target_pairs={{0,4},{4,0},{8,12},{12,8},{16,20},{20,16},{24,28},{28,24},{1,5},{5... | collective-permute-start | bytes 884744 | tf_op jit(solution)/shard_map/ppermute | solution.py:436
  10.2 2.5 %convolution_convert_fusion = bf16[1024,512]{1,0:T(8,128)(2,1)S(1)} fusion(bf16[1024,1024]{1,0:T(8,128)(2,1)S(1)} %copy-done, bf16[1024,512]{1,0:T(8,128)(2,1)} %param.25), kind=kOutput, calls=%fused_computation.1 | convolution fusion | flops 1074266112 | bytes 4194304 | tf_op jit(solution)/shard_map/dot_general | solution.py:482
  12.8 1.3 %convolution_bitcast_fusion.refs_3_.refs_5_ = f32[1024,512]{1,0:T(8,128)S(1)} fusion(bf16[1024,512]{1,0:T(8,128)(2,1)S(1)} %convolution_convert_fusion, bf16[1024,1024]{1,0:T(8,128)(2,1)S(1)} %copy-done), kind=kOutput, calls=%fused_computation | convolution fusion | flops 1073741824 | bytes 5242880 | tf_op jit(solution)/shard_map/dot_general | solution.py:25
  14.2 1.6 %collective-permute-start.11 = (f32[2,64,512]{2,1,0:T(8,128)S(1)}, f32[2,64,512]{2,1,0:T(8,128)S(1)}, u32[]{:S(2)}, u32[]{:S(2)}) collective-permute-start(f32[2,64,512]{2,1,0:T(8,128)S(1)} %join.2.refs_4_.refs_0_), channel_id=1, source_target_pairs={{0,8},{4,12},{8,0},{12,4},{16,24},{20,28},{24,16},{28,20},{1,9},{5... | collective-permute-start | bytes 786440 | tf_op jit(solution)/shard_map/ppermute | solution.py:436
  15.9 1.5 %collective-permute-done.refs_2_ = f32[64,1152]{1,0:T(8,128)S(1)} collective-permute-done((f32[64,1152]{1,0:T(8,128)}, f32[64,1152]{1,0:T(8,128)S(1)}, u32[]{:S(2)}, u32[]{:S(2)}) %collective-permute-start) | collective-permute-done | bytes 294944 | tf_op jit(solution)/shard_map/ppermute | solution.py:436
  17.8 1.9 %collective-permute-start.2 = (f32[64,256]{1,0:T(8,128)S(1)}, f32[64,256]{1,0:T(8,128)S(1)}, u32[]{:S(2)}, u32[]{:S(2)}) collective-permute-start(f32[64,256]{1,0:T(8,128)S(1)} %get-tuple-element.51), channel_id=1, source_target_pairs={{0,24},{4,28},{8,16},{12,20},{16,8},{20,12},{24,0},{28,4},{1,25},{... | collective-permute-start | bytes 196616 | tf_op jit(solution)/shard_map/ppermute | solution.py:436
  20.9 1.3 %collective-permute-start.4 = (f32[64,256]{1,0:T(8,128)S(1)}, f32[64,256]{1,0:T(8,128)S(1)}, u32[]{:S(2)}, u32[]{:S(2)}) collective-permute-start(f32[64,256]{1,0:T(8,128)S(1)} %get-tuple-element.53), channel_id=1, source_target_pairs={{0,8},{4,12},{8,0},{12,4},{16,24},{20,28},{24,16},{28,20},{1,9},{5... | collective-permute-start | bytes 196616 | tf_op jit(solution)/shard_map/ppermute | solution.py:436
  22.2 1.6 %band.2 = (f32[1024,512]{1,0:T(8,128)S(1)}, bf16[2,1024,192]{2,1,0:T(8,128)(2,1)S(1)}, f32[64,512]{1,0:T(8,128)S(1)}, f32[64,128]{1,0:T(8,128)S(1)}, f32[64,1024]{1,0:T(8,128)S(1)}) custom-call(bf16[2,1024,1024]{2,1,0:T(8,128)(2,1)S(1)} %copy-done.1, bf16[2,1024,512]{2,1,0:T(8,128)(2,1)S(1)} %copy-done.2, bf16[2,128,1024]{2,1,0:T(8,128)(2,1)S(1)} %pad_maximum_fusion.refs_2_, ...), custom_call_target="tpu_custom_call" | custom-call | flops 2000000000 | bytes 1000000 | tf_op jit(solution)/shard_map/band/pallas_call | solution.py:47
  23.9 1.6 %band.3 = (f32[1024,512]{1,0:T(8,128)S(1)}, bf16[2,1024,192]{2,1,0:T(8,128)(2,1)S(1)}, f32[64,512]{1,0:T(8,128)S(1)}, f32[64,128]{1,0:T(8,128)S(1)}, f32[64,1024]{1,0:T(8,128)S(1)}) custom-call(bf16[2,1024,1024]{2,1,0:T(8,128)(2,1)S(1)} %copy-done.1, bf16[2,1024,512]{2,1,0:T(8,128)(2,1)S(1)} %copy-done.2, bf16[2,128,1024]{2,1,0:T(8,128)(2,1)S(1)} %pad_maximum_fusion.refs_2_, ...), custom_call_target="tpu_custom_call" | custom-call | flops 2000000000 | bytes 1000000 | tf_op jit(solution)/shard_map/band/pallas_call | solution.py:47
  26.8 1.9 %collective-permute-start.7 = (f32[64,256]{1,0:T(8,128)S(1)}, f32[64,256]{1,0:T(8,128)S(1)}, u32[]{:S(2)}, u32[]{:S(2)}) collective-permute-start(f32[64,256]{1,0:T(8,128)S(1)} %sum.1.refs_1_.refs_2_), channel_id=1, source_target_pairs={{0,24},{4,28},{8,16},{12,20},{16,8},{20,12},{24,0},{28,4},{1,25},{... | collective-permute-start | bytes 196616 | tf_op jit(solution)/shard_map/ppermute | solution.py:436
  29.1 2.2 %collective-permute-start.5 = (f32[64,256]{1,0:T(8,128)S(1)}, f32[64,256]{1,0:T(8,128)S(1)}, u32[]{:S(2)}, u32[]{:S(2)}) collective-permute-start(f32[64,256]{1,0:T(8,128)S(1)} %sum.1.refs_1_.refs_2_), channel_id=1, source_target_pairs={{0,8},{4,12},{8,0},{12,4},{16,24},{20,28},{24,16},{28,20},{1,9},{5... | collective-permute-start | bytes 196616 | tf_op jit(solution)/shard_map/ppermute | solution.py:436
  31.3 1.6 %collective-permute-start.12 = (f32[4,64,512]{2,1,0:T(8,128)S(1)}, f32[4,64,512]{2,1,0:T(8,128)S(1)}, u32[]{:S(2)}, u32[]{:S(2)}) collective-permute-start(f32[4,64,512]{2,1,0:T(8,128)S(1)} %join.3.refs_0_), channel_id=1, source_target_pairs={{0,4},{4,0},{8,12},{12,8},{16,20},{20,16},{24,28},{28,24},{1,5},{5... | collective-permute-start | bytes 1572872 | tf_op jit(solution)/shard_map/ppermute | solution.py:436
  33.0 1.4 %collective-permute-done.6.refs_3_ = f32[64,256]{1,0:T(8,128)S(1)} collective-permute-done((f32[64,256]{1,0:T(8,128)S(1)}, f32[64,256]{1,0:T(8,128)S(1)}, u32[]{:S(2)}, u32[]{:S(2)}) %collective-permute-start.6) | collective-permute-done | bytes 65568 | tf_op jit(solution)/shard_map/ppermute | solution.py:436
  35.0 1.9 %collective-permute-start.10 = (f32[64,128]{1,0:T(8,128)S(1)}, f32[64,128]{1,0:T(8,128)S(1)}, u32[]{:S(2)}, u32[]{:S(2)}) collective-permute-start(f32[64,128]{1,0:T(8,128)S(1)} %get-tuple-element.65.refs_3_), channel_id=1, source_target_pairs={{0,24},{4,28},{8,16},{12,20},{16,8},{20,12},{24,0},{28,4},{1,25},{... | collective-permute-start | bytes 98312 | tf_op jit(solution)/shard_map/ppermute | solution.py:436
  37.7 1.7 %collective-permute-start.8 = (f32[64,128]{1,0:T(8,128)S(1)}, f32[64,128]{1,0:T(8,128)S(1)}, u32[]{:S(2)}, u32[]{:S(2)}) collective-permute-start(f32[64,128]{1,0:T(8,128)S(1)} %get-tuple-element.65.refs_3_), channel_id=1, source_target_pairs={{0,8},{4,12},{8,0},{12,4},{16,24},{20,28},{24,16},{28,20},{1,9},{5... | collective-permute-start | bytes 98312 | tf_op jit(solution)/shard_map/ppermute | solution.py:436
  39.5 2.9 %factor.1 = (f32[64,64]{1,0:T(8,128)S(1)}, f32[64,64]{1,0:T(8,128)S(1)}, f32[64,64]{1,0:T(8,128)S(1)}) custom-call(f32[64,64]{1,0:T(8,128)S(1)} %get-tuple-element.60.refs_0_, f32[64,1024]{1,0:T(8,128)S(1)} %get-tuple-element.59.refs_1_, f32[64,1024]{1,0:T(8,128)S(1)} %get-tuple-element.46.refs_5_.refs_2_, f32[64,1024]{1,0:T(8,128)S(1)} %get-tuple-element.61.refs_3_), custom_call_target="tpu_custom_call" | custom-call | flops 30000001024 | bytes 1000000 | tf_op jit(solution)/shard_map/factor/pallas_call | solution.py:47
  42.6 1.6 %collective-permute-start.14 = (f32[64,640]{1,0:T(8,128)S(1)}, f32[64,640]{1,0:T(8,128)S(1)}, u32[]{:S(2)}, u32[]{:S(2)}) collective-permute-start(f32[64,640]{1,0:T(8,128)S(1)} %scaled.1.refs_2_.refs_9_), channel_id=1, source_target_pairs={{0,4},{4,0},{8,12},{12,8},{16,20},{20,16},{24,28},{28,24},{1,5},{5... | collective-permute-start | bytes 491528 | tf_op jit(solution)/shard_map/ppermute | solution.py:436
  45.9 2.2 %collective-permute-done.14.refs_0_ = f32[64,640]{1,0:T(8,128)S(1)} collective-permute-done((f32[64,640]{1,0:T(8,128)S(1)}, f32[64,640]{1,0:T(8,128)S(1)}, u32[]{:S(2)}, u32[]{:S(2)}) %collective-permute-start.14) | collective-permute-done | bytes 163872 | tf_op jit(solution)/shard_map/ppermute | solution.py:436
  49.5 1.4 %collective-permute-done.17.refs_2_ = f32[64,640]{1,0:T(8,128)S(1)} collective-permute-done((f32[64,640]{1,0:T(8,128)S(1)}, f32[64,640]{1,0:T(8,128)S(1)}, u32[]{:S(2)}, u32[]{:S(2)}) %collective-permute-start.17) | collective-permute-done | bytes 163872 | tf_op jit(solution)/shard_map/ppermute | solution.py:439
  51.1 1.7 %collective-permute-start.18 = (f32[64,512]{1,0:T(8,128)S(1)}, f32[64,512]{1,0:T(8,128)S(1)}, u32[]{:S(2)}, u32[]{:S(2)}) collective-permute-start(f32[64,512]{1,0:T(8,128)S(1)} %slice.3), channel_id=1, source_target_pairs={{0,2},{1,3},{2,0},{3,1},{4,6},{5,7},{6,4},{7,5},{8,10},{9,11},{10,... | collective-permute-start | bytes 393224 | tf_op jit(solution)/shard_map/ppermute | solution.py:439
  53.7 2.5 %partial.1 = (f32[2,1024,512]{2,1,0:T(8,128)S(1)}, f32[2,64,512]{2,1,0:T(8,128)S(1)}, f32[2,64,128]{2,1,0:T(8,128)}) custom-call(f32[1024,512]{1,0:T(8,128)S(1)} %get-tuple-element.45.refs_0_, f32[1024,512]{1,0:T(8,128)S(1)} %get-tuple-element.47.refs_1_, bf16[2,1024,192]{2,1,0:T(8,128)(2,1)S(1)} %get-tuple-element.48.refs_2_.refs_0_, ...), custom_call_target="tpu_custom_call" | custom-call | flops 1000000000 | bytes 1000000 | tf_op jit(solution)/shard_map/partial/pallas_call | solution.py:47
  56.7 2.6 %finish.1 = (bf16[2,1024,512]{2,1,0:T(8,128)(2,1)}, f32[2,64,512]{2,1,0:T(8,128)}) custom-call(bf16[2,1024,192]{2,1,0:T(8,128)(2,1)S(1)} %get-tuple-element.48.refs_2_.refs_0_, bf16[2,1024,192]{2,1,0:T(8,128)(2,1)S(1)} %get-tuple-element.49.refs_3_.refs_1_, f32[64,128]{1,0:T(8,128)S(1)} %get-tuple-element.56.refs_2_.refs_0_, ...), custom_call_target="tpu_custom_call" | custom-call | flops 1000000000 | bytes 1000000 | tf_op jit(solution)/shard_map/finish/pallas_call | solution.py:602
  (66 shorter events, 10.7 us)
Async XLA Ops:
  0.6 9.6 %copy-start = (bf16[1024,1024]{1,0:T(8,128)(2,1)S(1)}, bf16[1024,1024]{1,0:T(8,128)(2,1)}, u32[]{:S(2)}) copy-start(bf16[1024,1024]{1,0:T(8,128)(2,1)} %param.21) | copy-start | bytes 6291460
  1.7 12.4 %collective-permute-start.1 = (f32[1,64,512]{2,1,0:T(8,128)S(1)}, f32[1,64,512]{2,1,0:T(8,128)S(1)}, u32[]{:S(2)}, u32[]{:S(2)}) collective-permute-start(f32[1,64,512]{2,1,0:T(8,128)S(1)} %widen.1.ready.refs_0_), channel_id=1, source_target_pairs={{0,16},{4,20},{8,24},{12,28},{16,0},{20,4},{24,8},{28,12},{1,17},{... | collective-permute-start | bytes 393224 | tf_op jit(solution)/shard_map/ppermute | solution.py:436
  8.6 8.7 %collective-permute-start = (f32[64,1152]{1,0:T(8,128)}, f32[64,1152]{1,0:T(8,128)S(1)}, u32[]{:S(2)}, u32[]{:S(2)}) collective-permute-start(f32[64,1152]{1,0:T(8,128)} %get-tuple-element.43.refs_1_), channel_id=1, source_target_pairs={{0,4},{4,0},{8,12},{12,8},{16,20},{20,16},{24,28},{28,24},{1,5},{5... | collective-permute-start | bytes 884744 | tf_op jit(solution)/shard_map/ppermute | solution.py:436
  12.7 4.6 %copy-start.8 = (f32[64,1152]{1,0:T(8,128)S(1)}, f32[64,1152]{1,0:T(8,128)}, u32[]{:S(2)}) copy-start(f32[64,1152]{1,0:T(8,128)} %get-tuple-element.43.refs_1_) | copy-start | bytes 884740
  12.8 9.5 %copy-start.2 = (bf16[2,1024,512]{2,1,0:T(8,128)(2,1)S(1)}, bf16[2,1024,512]{2,1,0:T(8,128)(2,1)}, u32[]{:S(2)}) copy-start(bf16[2,1024,512]{2,1,0:T(8,128)(2,1)} %refs_1_.3) | copy-start | bytes 6291460
  14.1 8.1 %copy-start.1 = (bf16[2,1024,1024]{2,1,0:T(8,128)(2,1)S(1)}, bf16[2,1024,1024]{2,1,0:T(8,128)(2,1)}, u32[]{:S(2)}) copy-start(bf16[2,1024,1024]{2,1,0:T(8,128)(2,1)} %refs_0_.5) | copy-start | bytes 12582916
  14.2 8.1 %copy-start.5 = (bf16[2,1024,64]{1,2,0:T(8,128)(2,1)S(1)}, bf16[2,1024,64]{1,2,0:T(8,128)(2,1)}, u32[]{:S(2)}) copy-start(bf16[2,1024,64]{1,2,0:T(8,128)(2,1)} %param.24) | copy-start | bytes 786436
  14.2 17.1 %collective-permute-start.11 = (f32[2,64,512]{2,1,0:T(8,128)S(1)}, f32[2,64,512]{2,1,0:T(8,128)S(1)}, u32[]{:S(2)}, u32[]{:S(2)}) collective-permute-start(f32[2,64,512]{2,1,0:T(8,128)S(1)} %join.2.refs_4_.refs_0_), channel_id=1, source_target_pairs={{0,8},{4,12},{8,0},{12,4},{16,24},{20,28},{24,16},{28,20},{1,9},{5... | collective-permute-start | bytes 786440 | tf_op jit(solution)/shard_map/ppermute | solution.py:436
  17.8 9.0 %collective-permute-start.2 = (f32[64,256]{1,0:T(8,128)S(1)}, f32[64,256]{1,0:T(8,128)S(1)}, u32[]{:S(2)}, u32[]{:S(2)}) collective-permute-start(f32[64,256]{1,0:T(8,128)S(1)} %get-tuple-element.51), channel_id=1, source_target_pairs={{0,24},{4,28},{8,16},{12,20},{16,8},{20,12},{24,0},{28,4},{1,25},{... | collective-permute-start | bytes 196616 | tf_op jit(solution)/shard_map/ppermute | solution.py:436
  19.7 7.1 %collective-permute-start.3 = (f32[64,256]{1,0:T(8,128)S(1)}, f32[64,256]{1,0:T(8,128)S(1)}, u32[]{:S(2)}, u32[]{:S(2)}) collective-permute-start(f32[64,256]{1,0:T(8,128)S(1)} %get-tuple-element.52), channel_id=1, source_target_pairs={{0,16},{4,20},{8,24},{12,28},{16,0},{20,4},{24,8},{28,12},{1,17},{... | collective-permute-start | bytes 196616 | tf_op jit(solution)/shard_map/ppermute | solution.py:436
  20.9 5.9 %collective-permute-start.4 = (f32[64,256]{1,0:T(8,128)S(1)}, f32[64,256]{1,0:T(8,128)S(1)}, u32[]{:S(2)}, u32[]{:S(2)}) collective-permute-start(f32[64,256]{1,0:T(8,128)S(1)} %get-tuple-element.53), channel_id=1, source_target_pairs={{0,8},{4,12},{8,0},{12,4},{16,24},{20,28},{24,16},{28,20},{1,9},{5... | collective-permute-start | bytes 196616 | tf_op jit(solution)/shard_map/ppermute | solution.py:436
  26.8 6.1 %collective-permute-start.7 = (f32[64,256]{1,0:T(8,128)S(1)}, f32[64,256]{1,0:T(8,128)S(1)}, u32[]{:S(2)}, u32[]{:S(2)}) collective-permute-start(f32[64,256]{1,0:T(8,128)S(1)} %sum.1.refs_1_.refs_2_), channel_id=1, source_target_pairs={{0,24},{4,28},{8,16},{12,20},{16,8},{20,12},{24,0},{28,4},{1,25},{... | collective-permute-start | bytes 196616 | tf_op jit(solution)/shard_map/ppermute | solution.py:436
  28.8 5.6 %collective-permute-start.6 = (f32[64,256]{1,0:T(8,128)S(1)}, f32[64,256]{1,0:T(8,128)S(1)}, u32[]{:S(2)}, u32[]{:S(2)}) collective-permute-start(f32[64,256]{1,0:T(8,128)S(1)} %sum.1.refs_1_.refs_2_), channel_id=1, source_target_pairs={{0,16},{4,20},{8,24},{12,28},{16,0},{20,4},{24,8},{28,12},{1,17},{... | collective-permute-start | bytes 196616 | tf_op jit(solution)/shard_map/ppermute | solution.py:436
  29.1 5.3 %collective-permute-start.5 = (f32[64,256]{1,0:T(8,128)S(1)}, f32[64,256]{1,0:T(8,128)S(1)}, u32[]{:S(2)}, u32[]{:S(2)}) collective-permute-start(f32[64,256]{1,0:T(8,128)S(1)} %sum.1.refs_1_.refs_2_), channel_id=1, source_target_pairs={{0,8},{4,12},{8,0},{12,4},{16,24},{20,28},{24,16},{28,20},{1,9},{5... | collective-permute-start | bytes 196616 | tf_op jit(solution)/shard_map/ppermute | solution.py:436
  31.3 12.9 %collective-permute-start.12 = (f32[4,64,512]{2,1,0:T(8,128)S(1)}, f32[4,64,512]{2,1,0:T(8,128)S(1)}, u32[]{:S(2)}, u32[]{:S(2)}) collective-permute-start(f32[4,64,512]{2,1,0:T(8,128)S(1)} %join.3.refs_0_), channel_id=1, source_target_pairs={{0,4},{4,0},{8,12},{12,8},{16,20},{20,16},{24,28},{28,24},{1,5},{5... | collective-permute-start | bytes 1572872 | tf_op jit(solution)/shard_map/ppermute | solution.py:436
  35.0 7.4 %collective-permute-start.10 = (f32[64,128]{1,0:T(8,128)S(1)}, f32[64,128]{1,0:T(8,128)S(1)}, u32[]{:S(2)}, u32[]{:S(2)}) collective-permute-start(f32[64,128]{1,0:T(8,128)S(1)} %get-tuple-element.65.refs_3_), channel_id=1, source_target_pairs={{0,24},{4,28},{8,16},{12,20},{16,8},{20,12},{24,0},{28,4},{1,25},{... | collective-permute-start | bytes 98312 | tf_op jit(solution)/shard_map/ppermute | solution.py:436
  36.9 5.5 %collective-permute-start.9 = (f32[64,128]{1,0:T(8,128)S(1)}, f32[64,128]{1,0:T(8,128)S(1)}, u32[]{:S(2)}, u32[]{:S(2)}) collective-permute-start(f32[64,128]{1,0:T(8,128)S(1)} %get-tuple-element.65.refs_3_), channel_id=1, source_target_pairs={{0,16},{4,20},{8,24},{12,28},{16,0},{20,4},{24,8},{28,12},{1,17},{... | collective-permute-start | bytes 98312 | tf_op jit(solution)/shard_map/ppermute | solution.py:436
  37.7 4.7 %collective-permute-start.8 = (f32[64,128]{1,0:T(8,128)S(1)}, f32[64,128]{1,0:T(8,128)S(1)}, u32[]{:S(2)}, u32[]{:S(2)}) collective-permute-start(f32[64,128]{1,0:T(8,128)S(1)} %get-tuple-element.65.refs_3_), channel_id=1, source_target_pairs={{0,8},{4,12},{8,0},{12,4},{16,24},{20,28},{24,16},{28,20},{1,9},{5... | collective-permute-start | bytes 98312 | tf_op jit(solution)/shard_map/ppermute | solution.py:436
  42.6 5.6 %collective-permute-start.14 = (f32[64,640]{1,0:T(8,128)S(1)}, f32[64,640]{1,0:T(8,128)S(1)}, u32[]{:S(2)}, u32[]{:S(2)}) collective-permute-start(f32[64,640]{1,0:T(8,128)S(1)} %scaled.1.refs_2_.refs_9_), channel_id=1, source_target_pairs={{0,4},{4,0},{8,12},{12,8},{16,20},{20,16},{24,28},{28,24},{1,5},{5... | collective-permute-start | bytes 491528 | tf_op jit(solution)/shard_map/ppermute | solution.py:436
  44.2 3.9 %collective-permute-start.15 = (f32[4,64,512]{2,1,0:T(8,128)S(1)}, f32[4,64,512]{2,1,0:T(8,128)S(1)}, u32[]{:S(2)}, u32[]{:S(2)}) collective-permute-start(f32[4,64,512]{2,1,0:T(8,128)S(1)} %join.3.refs_0_), channel_id=1, source_target_pairs={{0,1},{1,0},{2,3},{3,2},{4,5},{5,4},{6,7},{7,6},{8,9},{9,8},{10,11... | collective-permute-start | bytes 1572872 | tf_op jit(solution)/shard_map/ppermute | solution.py:439
  44.3 3.9 %collective-permute-start.16 = (f32[4,64,512]{2,1,0:T(8,128)S(1)}, f32[4,64,512]{2,1,0:T(8,128)S(1)}, u32[]{:S(2)}, u32[]{:S(2)}) collective-permute-start(f32[4,64,512]{2,1,0:T(8,128)S(1)} %held.2.refs_3_.refs_1_), channel_id=1, source_target_pairs={{0,1},{1,0},{2,3},{3,2},{4,5},{5,4},{6,7},{7,6},{8,9},{9,8},{10,11... | collective-permute-start | bytes 1572872 | tf_op jit(solution)/shard_map/ppermute | solution.py:439
  45.4 8.3 %collective-permute-start.13 = (f32[64,1024]{1,0:T(8,128)S(1)}, f32[64,1024]{1,0:T(8,128)S(1)}, u32[]{:S(2)}, u32[]{:S(2)}) collective-permute-start(f32[64,1024]{1,0:T(8,128)S(1)} %spread.1.refs_4_), channel_id=1, source_target_pairs={{0,4},{4,0},{8,12},{12,8},{16,20},{20,16},{24,28},{28,24},{1,5},{5... | collective-permute-start | bytes 786440 | tf_op jit(solution)/shard_map/ppermute | solution.py:436
  49.4 1.5 %collective-permute-start.17 = (f32[64,640]{1,0:T(8,128)S(1)}, f32[64,640]{1,0:T(8,128)S(1)}, u32[]{:S(2)}, u32[]{:S(2)}) collective-permute-start(f32[64,640]{1,0:T(8,128)S(1)} %get-tuple-element.72.refs_0_.refs_1_), channel_id=1, source_target_pairs={{0,1},{1,0},{2,3},{3,2},{4,5},{5,4},{6,7},{7,6},{8,9},{9,8},{10,11... | collective-permute-start | bytes 491528 | tf_op jit(solution)/shard_map/ppermute | solution.py:439
  51.1 5.6 %collective-permute-start.18 = (f32[64,512]{1,0:T(8,128)S(1)}, f32[64,512]{1,0:T(8,128)S(1)}, u32[]{:S(2)}, u32[]{:S(2)}) collective-permute-start(f32[64,512]{1,0:T(8,128)S(1)} %slice.3), channel_id=1, source_target_pairs={{0,2},{1,3},{2,0},{3,1},{4,6},{5,7},{6,4},{7,5},{8,10},{9,11},{10,... | collective-permute-start | bytes 393224 | tf_op jit(solution)/shard_map/ppermute | solution.py:439
  (9 other events, 18.8 us)
